TPU v7x, 32 devices: a whole 2x2x4 slice. The times are simulated.
32 devices in a mesh: dp: 8 (over z, x), fsdp: 4 (over y, core).
Axes of the slice: x: 2, y: 2, z: 4, core: 2. Of those that a mesh axis runs over, the one named last changes fastest.
Arguments:
- inputs: bfloat16 [64, 529, 768], P(('dp', 'fsdp')), may hold values from -6 to 6
- row_kind: int32 [64], P(('dp', 'fsdp')), may hold values from 0 to 1
- ln1_gain: bfloat16 [768], P(('dp', 'fsdp')), may hold values from 0.25 to 1.75
- ln1_bias: bfloat16 [768], P(('dp', 'fsdp')), may hold values from -1.75 to 1.75
- w_qkv: bfloat16 [768, 2304], P(('dp', 'fsdp')), may hold values from -0.21875 to 0.21875
- b_query: bfloat16 [768], P(('dp', 'fsdp')), may hold values from -3 to 3
- b_value: bfloat16 [768], P(('dp', 'fsdp')), may hold values from -3 to 3
- w_out: bfloat16 [768, 768], P(('dp', 'fsdp')), may hold values from -1.75 to 1.75
- b_out: bfloat16 [768], P(('dp', 'fsdp')), may hold values from -1.75 to 1.75
- ln2_gain: bfloat16 [768], P(('dp', 'fsdp')), may hold values from 0.25 to 1.75
- ln2_bias: bfloat16 [768], P(('dp', 'fsdp')), may hold values from -1.75 to 1.75
- w_up: bfloat16 [768, 3072], P(('dp', 'fsdp')), may hold values from -0.21875 to 0.21875
- b_up: bfloat16 [3072], P(('dp', 'fsdp')), may hold values from -3 to 3
- w_down: bfloat16 [3072, 768], P(('dp', 'fsdp')), may hold values from -0.109375 to 0.109375
- b_down: bfloat16 [768], P(('dp', 'fsdp')), may hold values from -1.75 to 1.75
- out_grad: bfloat16 [64, 529, 768], P(('dp', 'fsdp')), may hold values from -6 to 6
Outputs:
- outputs: bfloat16 [64, 529, 768], P(('dp', 'fsdp'))
- input_grad: bfloat16 [64, 529, 768], P(('dp', 'fsdp'))
- grad_ln1_gain: float32 [768], P(('dp', 'fsdp'))
- grad_ln1_bias: float32 [768], P(('dp', 'fsdp'))
- grad_w_qkv: float32 [768, 2304], P(('dp', 'fsdp'))
- grad_b_query: float32 [768], P(('dp', 'fsdp'))
- grad_b_value: float32 [768], P(('dp', 'fsdp'))
- grad_w_out: float32 [768, 768], P(('dp', 'fsdp'))
- grad_b_out: float32 [768], P(('dp', 'fsdp'))
- grad_ln2_gain: float32 [768], P(('dp', 'fsdp'))
- grad_ln2_bias: float32 [768], P(('dp', 'fsdp'))
- grad_w_up: float32 [768, 3072], P(('dp', 'fsdp'))
- grad_b_up: float32 [3072], P(('dp', 'fsdp'))
- grad_w_down: float32 [3072, 768], P(('dp', 'fsdp'))
- grad_b_down: float32 [768], P(('dp', 'fsdp'))
Inputs may be any that keep to these rules, and one draw needn't show every extreme that they name: `row_kind`: 0 marks a row holding one strip of 529 patches; 1 marks a row holding two half strips of 264 patches followed by one padding slot.
All inputs are finite; a program needn't handle non-finite values.
Results may differ from a plain program's by a relative error of at most 0.012.
Values may be sent and summed in bfloat16 or wider, within the bound.
A program may use at most 256 MiB of HBM per device.

v0:
```python
import functools
import math

import jax
import jax.numpy as jnp
from jax import lax
from jax.experimental import pallas as pl
from jax.experimental.pallas import tpu as pltpu
from jax.sharding import PartitionSpec as P

D = 768
HD = 64
FF = 3072
SEQ = 529
HALF = 264
EPS = 1e-06
S = 544
T = 2 * S
MB = 272
HG = 4
QW = HG * HD
GW = 3 * QW
FC = 512
OUT_AT = 3 * D
UP_AT = 4 * D
AW = 4 * D + FF
F32 = jnp.float32
BF = jnp.bfloat16
LIMIT = 62 * 2**20
MESH = pl.DeviceIdType.MESH
NN = (((1,), (0,)), ((), ()))
NT = (((1,), (1,)), ((), ()))
TN = (((0,), (0,)), ((), ()))


def mm(a, b, dims=NN):
    return lax.dot_general(a, b, dims, preferred_element_type=F32)


def norm_parts(values):
    mean = jnp.mean(values, -1, keepdims=True)
    centred = values - mean
    inverse = lax.rsqrt(jnp.mean(centred * centred, -1, keepdims=True) + EPS)
    return centred * inverse, inverse


def norm_pull(grad, normed, inverse, gain):
    scaled = grad * gain
    return inverse * (
        scaled
        - jnp.mean(scaled, -1, keepdims=True)
        - normed * jnp.mean(scaled * normed, -1, keepdims=True)
    )


def gelu_both(u):
    a = jnp.abs(u)
    t = 1.0 / (1.0 + (0.3275911 / math.sqrt(2.0)) * a)
    e = jnp.exp(-0.5 * u * u)
    poly = t * (
        0.254829592
        + t * (-0.284496736 + t * (1.421413741 + t * (-1.453152027 + t * 1.061405429)))
    )
    tail = 0.5 * poly * e
    phi = jnp.where(u < 0, tail, 1.0 - tail)
    return u * phi, phi + u * e * (1.0 / math.sqrt(2.0 * math.pi))


def head_lanes(shape, e):
    lane = lax.broadcasted_iota(jnp.int32, shape, 1)
    return (lane // HD) == e


def whole(shape):
    return pl.BlockSpec(shape, lambda *_: (0,) * len(shape))


def rows_of(i):
    return pl.ds(pl.multiple_of(i * MB, 16), MB)


def row_of(i):
    return pl.ds(pl.multiple_of(i * S, 16), S)


G1, B1, BQ, BV, BO, G2, B2, BD = range(8)


def attn_fwd_kernel(
    kind_ref, x_ref, wg_ref, bqkv_ref, wo_ref, vec_ref,
    h1_ref, qkv_ref, p_ref, attn_ref, rl_ref, x1_ref, fa, fb,
):
    hq, r = pl.program_id(0), pl.program_id(1)

    @pl.when((hq == 0) & (r == 0))
    def _():
        for row in range(2):
            h1_ref[pl.ds(row * S + S - 16, 16), :] = jnp.zeros((16, D), BF)
            n1, _s = norm_parts(x_ref[row].astype(F32))
            h1_ref[pl.ds(row * S, SEQ), :] = (n1 * vec_ref[G1:G1 + 1, :] + vec_ref[B1:B1 + 1, :]).astype(BF)
            slot = lax.broadcasted_iota(jnp.int32, (S, 128), 0)
            lane = lax.broadcasted_iota(jnp.int32, (S, 128), 1)
            packed = jnp.where(slot < HALF, 0, jnp.where(slot < 2 * HALF, 1, 2))
            seg = jnp.where(kind_ref[row] == 1, packed, 0)
            fa[row] = jnp.where((lane < 3) & (seg == lane), -1e30, 0.0).astype(BF)
            fb[row] = jnp.where((lane < 3) & ((seg != lane) | (slot >= SEQ)), 1.0, 0.0).astype(BF)

    @pl.when(r == 0)
    def _():
        @pl.loop(0, T // MB)
        def _(i):
            rows = rows_of(i)
            qkv_ref[rows, :] = (mm(h1_ref[rows, :], wg_ref[...]) + bqkv_ref[...]).astype(BF)

    rows = pl.ds(pl.multiple_of(r * S, 16), S)
    feat_q, feat_k = fa[r], fb[r]
    ones = jnp.ones((S, 128), BF)
    scale = math.log2(math.e) / math.sqrt(HD)
    for j in range(HG // 2):
        at = j * 384
        qp, kp, vp = (qkv_ref[rows, at + 128 * n: at + 128 * (n + 1)] for n in range(3))
        kcat = jnp.concatenate([kp, feat_k], 1)
        total = None
        inv = None
        for e in range(2):
            keep = head_lanes((S, 128), e)
            qcat = jnp.concatenate([jnp.where(keep, qp, jnp.zeros_like(qp)), feat_q], 1)
            s = mm(qcat, kcat, NT)
            m = jnp.max(s, -1, keepdims=True)
            pb = jnp.exp2((s - m) * scale).astype(BF)
            p_ref[0, 2 * j + e] = pb
            vcat = jnp.concatenate([jnp.where(keep, vp, jnp.zeros_like(vp)), ones], 1)
            o = mm(pb, vcat)
            rl = 1.0 / o[:, 128:]
            part = o[:, :128] * rl
            total = part if total is None else total + part
            inv = rl if inv is None else jnp.where(keep, rl, inv)
        out = pl.ds(pl.multiple_of(hq * QW + j * 128, 128), 128)
        attn_ref[rows, out] = total.astype(BF)
        rl_ref[rows, out] = inv

    @pl.when((hq == D // QW - 1) & (r == 1))
    def _():
        for row in range(2):
            x1_ref[pl.ds(row * S + S - 16, 16), :] = jnp.zeros((16, D), F32)
            x1_ref[pl.ds(row * S, SEQ), :] = x_ref[row].astype(F32)

        @pl.loop(0, T // MB)
        def _(i):
            rr = rows_of(i)
            x1_ref[rr, :] = x1_ref[rr, :] + mm(attn_ref[rr, :], wo_ref[...]) + vec_ref[BO:BO + 1, :]


def attn_fwd(kind, x, wide, bqkv, vec):
    return pl.pallas_call(
        attn_fwd_kernel,
        grid=(D // QW, 2),
        in_specs=[
            pl.BlockSpec(memory_space=pltpu.SMEM), whole((2, SEQ, D)),
            pl.BlockSpec((D, GW), lambda h, r: (0, h)), pl.BlockSpec((1, GW), lambda h, r: (0, h)),
            pl.BlockSpec((D, D), lambda h, r: (0, 3)), whole((8, D)),
        ],
        out_specs=[
            whole((T, D)), pl.BlockSpec((T, GW), lambda h, r: (0, h)),
            pl.BlockSpec((1, HG, S, S), lambda h, r: (r, h, 0, 0)),
            whole((T, D)), whole((T, D)), whole((T, D)),
        ],
        out_shape=[
            jax.ShapeDtypeStruct((T, D), BF), jax.ShapeDtypeStruct((T, 3 * D), BF),
            jax.ShapeDtypeStruct((2, D // HD, S, S), BF),
            jax.ShapeDtypeStruct((T, D), BF), jax.ShapeDtypeStruct((T, D), F32), jax.ShapeDtypeStruct((T, D), F32),
        ],
        scratch_shapes=[pltpu.VMEM((2, S, 128), BF), pltpu.VMEM((2, S, 128), BF)],
        compiler_params=pltpu.CompilerParams(vmem_limit_bytes=LIMIT),
        name="attention_forward",
    )(kind, x, wide, bqkv, wide, vec)


def ffn_kernel(
    x1_ref, dm_ref, wu_ref, wd_ref, bu_ref, vec_ref,
    out_ref, dx1_ref, gwu_ref, gwd_ref, gbu_ref, gg2_ref, gb2_ref, gbd_ref,
    h2, h2t, dm, yacc, dacc, gs, dus,
):
    c = pl.program_id(0)

    @pl.when(c == 0)
    def _():
        for row in range(2):
            dm[pl.ds(row * S + S - 16, 16), :] = jnp.zeros((16, D), BF)
            dm[pl.ds(row * S, SEQ), :] = dm_ref[row]

        @pl.loop(0, T // MB)
        def _(i):
            rows = rows_of(i)
            x1 = x1_ref[rows, :]
            n2, _s = norm_parts(x1)
            h2[rows, :] = (n2 * vec_ref[G2:G2 + 1, :] + vec_ref[B2:B2 + 1, :]).astype(BF)
            yacc[rows, :] = x1 + vec_ref[BD:BD + 1, :]
            dacc[rows, :] = jnp.zeros((MB, D), F32)
        h2t[...] = h2[...].T
        gbd_ref[...] = jnp.sum(dm[...].astype(F32), 0, keepdims=True)

    gbu_ref[...] = jnp.zeros_like(gbu_ref)

    @pl.loop(0, T // MB)
    def _(i):
        rows = rows_of(i)
        u = mm(h2[rows, :], wu_ref[...]) + bu_ref[...]
        g, slope = gelu_both(u)
        gb = g.astype(BF)
        gs[rows, :] = gb
        yacc[rows, :] += mm(gb, wd_ref[...])
        du = (mm(dm[rows, :], wd_ref[...], NT) * slope).astype(BF)
        dus[rows, :] = du
        gbu_ref[...] += jnp.sum(du.astype(F32), 0, keepdims=True)
        dacc[rows, :] += mm(du, wu_ref[...], NT)

    for t in range(FC // 256):
        cols = pl.ds(t * 256, 256)
        gwd_ref[cols, :] = mm(gs[:, cols], dm[...], TN).astype(BF)

    @pl.loop(0, D // 256)
    def _(t):
        rows = pl.ds(pl.multiple_of(t * 256, 256), 256)
        gwu_ref[rows, :] = mm(h2t[rows, :], dus[...]).astype(BF)

    @pl.when(c == FF // FC - 1)
    def _():
        gg2_ref[...] = jnp.zeros_like(gg2_ref)
        gb2_ref[...] = jnp.zeros_like(gb2_ref)
        for row in range(2):
            out_ref[row] = yacc[pl.ds(row * S, SEQ), :].astype(BF)

        @pl.loop(0, T // MB)
        def _(i):
            rows = rows_of(i)
            n2, s2 = norm_parts(x1_ref[rows, :])
            dh = dacc[rows, :]
            gg2_ref[...] += jnp.sum(dh * n2, 0, keepdims=True)
            gb2_ref[...] += jnp.sum(dh, 0, keepdims=True)
            dx1_ref[rows, :] = dm[rows, :].astype(F32) + norm_pull(dh, n2, s2, vec_ref[G2:G2 + 1, :])


def ffn(x1, dm, wide, down, bu, vec):
    one = jax.ShapeDtypeStruct((1, D), F32)
    return pl.pallas_call(
        ffn_kernel,
        grid=(FF // FC,),
        in_specs=[
            whole((T, D)), whole((2, SEQ, D)),
            pl.BlockSpec((D, FC), lambda c: (0, c + UP_AT // FC)), pl.BlockSpec((FC, D), lambda c: (c, 0)),
            pl.BlockSpec((1, FC), lambda c: (0, c)), whole((8, D)),
        ],
        out_specs=[
            whole((2, SEQ, D)), whole((T, D)),
            pl.BlockSpec((D, FC), lambda c: (0, c)), pl.BlockSpec((FC, D), lambda c: (c, 0)),
            pl.BlockSpec((1, FC), lambda c: (0, c)), whole((1, D)), whole((1, D)), whole((1, D)),
        ],
        out_shape=[
            jax.ShapeDtypeStruct((2, SEQ, D), BF), jax.ShapeDtypeStruct((T, D), F32),
            jax.ShapeDtypeStruct((D, FF), BF), jax.ShapeDtypeStruct((FF, D), BF),
            jax.ShapeDtypeStruct((1, FF), F32), one, one, one,
        ],
        scratch_shapes=[
            pltpu.VMEM((T, D), BF), pltpu.VMEM((D, T), BF), pltpu.VMEM((T, D), BF),
            pltpu.VMEM((T, D), F32), pltpu.VMEM((T, D), F32),
            pltpu.VMEM((T, FC), BF), pltpu.VMEM((T, FC), BF),
        ],
        compiler_params=pltpu.CompilerParams(vmem_limit_bytes=LIMIT),
        name="feed_forward",
    )(x1, dm, wide, down, bu, vec)


def attn_bwd_kernel(
    x_ref, dx1_ref, h1_ref, qkv_ref, p_ref, attn_ref, rl_ref, wo_ref, wqkv_ref, vec_ref,
    gx_ref, gwqkv_ref, gwo_ref, gbqkv_ref, gbo_ref, gg1_ref, gb1_ref,
    da, dos, h1t, dqkv,
):
    hq, r = pl.program_id(0), pl.program_id(1)

    @pl.when((hq == 0) & (r == 0))
    def _():
        gbo_ref[...] = jnp.zeros_like(gbo_ref)

        @pl.loop(0, T // MB)
        def _(i):
            rows = rows_of(i)
            d = dx1_ref[rows, :].astype(BF)
            da[rows, :] = d
            gbo_ref[...] += jnp.sum(d.astype(F32), 0, keepdims=True)
            dos[rows, :] = (mm(d, wo_ref[...], NT) * rl_ref[rows, :]).astype(BF)
        h1t[...] = h1_ref[...].T

    rows = pl.ds(pl.multiple_of(r * S, 16), S)
    scale = 1.0 / math.sqrt(HD)
    for j in range(HG // 2):
        at = j * 384
        qp, kp, vp = (qkv_ref[rows, at + 128 * n: at + 128 * (n + 1)] for n in range(3))
        do = dos[rows, pl.ds(pl.multiple_of(hq * QW + j * 128, 128), 128)]
        prod = do.astype(F32) * attn_ref[rows, j * 128:(j + 1) * 128].astype(F32)
        dq = dk = dv = None
        for e in range(2):
            keep = head_lanes((S, 128), e)
            zero = jnp.zeros_like(qp)
            doe = jnp.where(keep, do, zero)
            dot = jnp.sum(jnp.where(keep, prod, 0.0), -1, keepdims=True)
            p = p_ref[0, 2 * j + e]
            ds = (p.astype(F32) * (mm(doe, vp, NT) - dot)).astype(BF)
            a = mm(ds, jnp.where(keep, kp, zero))
            b = mm(ds, jnp.where(keep, qp, zero), TN)
            c = mm(p, doe, TN)
            dq, dk, dv = (a, b, c) if dq is None else (dq + a, dk + b, dv + c)
        for n, part in enumerate((dq * scale, dk * scale, dv)):
            col = hq * GW + j * 384 + n * 128
            dqkv[rows, pl.ds(pl.multiple_of(col, 128), 128)] = part.astype(BF)

    @pl.when(r == 1)
    def _():
        part = dqkv[:, pl.ds(pl.multiple_of(hq * GW, 128), GW)]
        gbqkv_ref[...] = jnp.sum(part.astype(F32), 0, keepdims=True)

        @pl.loop(0, D // 256)
        def _(t):
            rr = pl.ds(pl.multiple_of(t * 256, 256), 256)
            gwqkv_ref[rr, :] = mm(h1t[rr, :], part).astype(BF)
        gwo_ref[...] = mm(attn_ref[...], da[...], TN).astype(BF)

    @pl.when((hq == D // QW - 1) & (r == 1))
    def _():
        gg1_ref[...] = jnp.zeros_like(gg1_ref)
        gb1_ref[...] = jnp.zeros_like(gb1_ref)
        for row in range(2):
            rr = pl.ds(row * S, SEQ)
            dh = mm(dqkv[pl.ds(row * S, S), :], wqkv_ref[...], NT)[:SEQ]
            n1, s1 = norm_parts(x_ref[row].astype(F32))
            gg1_ref[...] += jnp.sum(dh * n1, 0, keepdims=True)
            gb1_ref[...] += jnp.sum(dh, 0, keepdims=True)
            gx_ref[row] = (dx1_ref[rr, :] + norm_pull(dh, n1, s1, vec_ref[G1:G1 + 1, :])).astype(BF)


def attn_bwd(x, dx1, h1, qkv, p, attn, rl, wide, vec):
    act = pl.BlockSpec((T, QW), lambda h, r: (0, h))
    one = jax.ShapeDtypeStruct((1, D), F32)
    return pl.pallas_call(
        attn_bwd_kernel,
        grid=(D // QW, 2),
        in_specs=[
            whole((2, SEQ, D)), whole((T, D)), whole((T, D)), pl.BlockSpec((T, GW), lambda h, r: (0, h)),
            pl.BlockSpec((1, HG, S, S), lambda h, r: (r, h, 0, 0)), act, whole((T, D)),
            pl.BlockSpec((D, D), lambda h, r: (0, 3)), whole((D, 3 * D)), whole((8, D)),
        ],
        out_specs=[
            whole((2, SEQ, D)), pl.BlockSpec((D, GW), lambda h, r: (0, h)),
            pl.BlockSpec((QW, D), lambda h, r: (h, 0)),
            pl.BlockSpec((1, GW), lambda h, r: (0, h)), whole((1, D)), whole((1, D)), whole((1, D)),
        ],
        out_shape=[
            jax.ShapeDtypeStruct((2, SEQ, D), BF), jax.ShapeDtypeStruct((D, 3 * D), BF), jax.ShapeDtypeStruct((D, D), BF),
            jax.ShapeDtypeStruct((1, 3 * D), F32), one, one, one,
        ],
        scratch_shapes=[
            pltpu.VMEM((T, D), BF), pltpu.VMEM((T, D), BF), pltpu.VMEM((D, T), BF), pltpu.VMEM((T, 3 * D), BF),
        ],
        compiler_params=pltpu.CompilerParams(vmem_limit_bytes=LIMIT),
        name="attention_backward",
    )(x, dx1, h1, qkv, p, attn, rl, wide, wide, vec)


NZ = 4
CH = 48
HW = 384
SR = 16
N_WIDE = AW // (2 * HW)
N_DOWN = 4
N_UP = FF // D
DH = 2 * CH
NV = 8
VW = (24,) * NV + (96,)


def one(i):
    return pl.ds(i, 1)


EVERY = pl.ds(0, NZ)
TWO = pl.ds(0, 2)


def where_am_i():
    dp, fs = lax.axis_index("dp"), lax.axis_index("fsdp")
    return lax.div(dp, 2), lax.rem(dp, 2), lax.div(fs, 2), lax.rem(fs, 2)


def device(z, x, y, c):
    return (z * 2 + x, y * 2 + c)


def partners(z, x, y, c):
    found = [device(lax.rem(z + k, NZ), x, y, c) for k in (1, 2, 3)]
    return found + [device(z, 1 - x, y, c), device(z, x, 1 - y, c), device(z, x, y, 1 - c)]


def say_hello(here):
    barrier = pltpu.get_barrier_semaphore()
    for other in partners(*here):
        pl.semaphore_signal(barrier, inc=1, device_id=other, device_id_type=MESH)


def await_all():
    pl.semaphore_wait(pltpu.get_barrier_semaphore(), 6)


def remote(src, dst, sems, n, target):
    return pltpu.make_async_remote_copy(
        src_ref=src, dst_ref=dst, send_sem=sems[0].at[n], recv_sem=sems[1].at[n],
        device_id=target, device_id_type=MESH,
    )


def half(i, core):
    return pl.ds(pl.multiple_of(i * 2 * HW + core * HW, 128), HW)


def down_rows(i, core):
    return pl.ds(pl.multiple_of(core * DH + (i // 2) * CH, 16), CH)


def down_cols(i):
    return pl.ds((i % 2) * HW, HW)


TOK = 48


def rows_in(src, row, *targets):
    for ref in targets:
        ref[pl.ds(row * S + S - 16, 16), :] = jnp.zeros((16, D), ref.dtype)

    @pl.loop(0, SEQ // TOK)
    def _(i):
        part = src[pl.ds(i * TOK, TOK), row, :]
        for ref in targets:
            ref[pl.ds(pl.multiple_of(row * S + i * TOK, 16), TOK), :] = part.astype(ref.dtype)
    last = src[SEQ - 1:SEQ, row, :]
    for ref in targets:
        ref[pl.ds(row * S + SEQ - 1, 1), :] = last.astype(ref.dtype)


def rows_out(src, target, row):
    @pl.loop(0, SEQ // TOK)
    def _(i):
        target[pl.ds(i * TOK, TOK), row, :] = src[pl.ds(pl.multiple_of(row * S + i * TOK, 16), TOK), :]
    target[SEQ - 1:SEQ, row, :] = src[pl.ds(row * S + SEQ - 1, 1), :]


def transpose_into(target, src):
    @pl.loop(0, D // 128)
    def _(i):
        cols = pl.ds(pl.multiple_of(i * 128, 128), 128)
        target[cols, :] = src[:, cols].T


def add(a, b):
    return (a.astype(F32) + b.astype(F32)).astype(BF)


def plan(entries, ticks):
    table = {n: [] for n in range(len(ticks))}
    rest = []
    for due, action in sorted(entries, key=lambda e: e[0]):
        slot = min((n for n, t in enumerate(ticks) if t >= due), default=None)
        (rest if slot is None else table[slot]).append(action)
    return table, rest


class Gather:
    COPIES = 7

    def __init__(self, here, sems, base, view, first):
        z, x, y, c = here
        peers = partners(*here)
        mine = view(one(z), one(x), one(y))
        column = view(EVERY, one(x), one(y))
        fx, fy = jnp.where(c == 0, 1 - x, x), jnp.where(c == 0, y, 1 - y)
        tx, ty = jnp.where(c == 0, x, 1 - x), jnp.where(c == 0, 1 - y, y)
        passed = view(EVERY, one(fx), one(fy))
        all_of = view(EVERY, TWO, TWO)
        make = lambda n, src, dst, to: remote(src, dst, sems, base + n, to)
        self.along_z = [make(k, mine if first is None else first, mine, peers[k]) for k in range(3)]
        self.along_x = make(3, column, column, peers[3])
        self.along_y = make(4, column, column, peers[4])
        self.diagonal = make(5, passed, passed, device(z, tx, ty, c))
        self.sibling = make(6, all_of, all_of, peers[5])

    def start(self, phase):
        if phase == 0:
            for copy in self.along_z:
                copy.start()
        elif phase == 1:
            for copy in self.along_z:
                copy.wait_recv()
            self.along_x.start()
            self.along_y.start()
        elif phase == 2:
            self.along_x.wait_recv()
            self.along_y.wait_recv()
            self.diagonal.start()
        elif phase == 3:
            self.diagonal.wait_recv()
            self.sibling.start()
        else:
            self.sibling.wait_recv()

    def drain(self):
        for copy in (*self.along_z, self.along_x, self.along_y, self.diagonal, self.sibling):
            copy.wait_send()


class Scatter:
    COPIES = 7

    def __init__(self, here, sems, base, theirs, mine, acc, via, last, zs):
        self.mine, self.acc, self.via, self.last, self.zs = mine, acc, via, last, zs
        z, x, y, c = self.here = here
        peers = partners(*here)
        ix, iy = jnp.where(c == 0, x, 1 - x), jnp.where(c == 0, 1 - y, y)
        self.px, self.py = jnp.where(c == 0, 1 - x, x), jnp.where(c == 0, y, 1 - y)
        first, second = device(z, ix, iy, c), device(z, self.px, self.py, c)
        make = lambda n, src, dst, to: remote(src, dst, sems, base + n, to)
        at = lambda xs, ys: acc.at[EVERY, one(xs), one(ys)]
        self.swap = make(0, theirs, acc, peers[5])
        self.far = make(1, at(1 - x, 1 - y), via.at[0], first)
        self.near = make(2, at(ix, iy), via.at[1], first)
        self.next = make(3, at(self.px, self.py), last, second)
        self.along_z = [
            make(4 + k, acc.at[one(lax.rem(z + k + 1, NZ)), one(x), one(y)], zs.at[k], peers[k]) for k in range(3)
        ]

    def start(self, phase):
        z, x, y, c = self.here
        acc = self.acc
        if phase == 0:
            self.swap.start()
        elif phase == 1:
            self.swap.wait_recv()

            @pl.loop(0, NZ)
            def _(i):
                for xi in range(2):
                    for yi in range(2):
                        acc[i, xi, yi] = add(acc[i, xi, yi], self.mine(i, xi, yi))
            self.far.start()
            self.near.start()
        elif phase == 2:
            self.far.wait_recv()
            px, py = self.px, self.py

            @pl.loop(0, NZ)
            def _(i):
                acc[i, px, py] = add(acc[i, px, py], self.via[0, i, 0, 0])
            self.next.start()
            self.near.wait_recv()

            @pl.loop(0, NZ)
            def _(i):
                acc[i, x, y] = add(acc[i, x, y], self.via[1, i, 0, 0])
        elif phase == 3:
            self.next.wait_recv()

            @pl.loop(0, NZ)
            def _(i):
                acc[i, x, y] = add(acc[i, x, y], self.last[i, 0, 0])
            for copy in self.along_z:
                copy.start()

    def total(self):
        z, x, y, c = self.here
        for copy in self.along_z:
            copy.wait_recv()
        parts = [self.acc[z, x, y]] + [self.zs[k, 0, 0, 0] for k in range(3)]
        return sum(part.astype(F32) for part in parts)

    def drain(self):
        for copy in (self.swap, self.far, self.near, self.next, *self.along_z):
            copy.wait_send()


def scatter_bufs(n, width):
    return [
        pltpu.VMEM((n, NZ, 2, 2, CH, width), BF), pltpu.VMEM((n, 2, NZ, 1, 1, CH, width), BF),
        pltpu.VMEM((n, NZ, 1, 1, CH, width), BF), pltpu.VMEM((n, 3, 1, 1, 1, CH, width), BF),
    ]


def dma_sems(*counts):
    return [pltpu.SemaphoreType.DMA((k,)) for k in counts]


def fixed(shape):
    return pl.BlockSpec(shape, lambda s: (0,) * len(shape), pipeline_mode=pl.Buffered(1))


def vmem():
    return pl.BlockSpec(memory_space=pltpu.VMEM)


def hbm():
    return pl.BlockSpec(memory_space=pl.ANY)


N_ATT = 2 * (D // QW)
PACE = 5.4
FORWARD_LAG = (0.0, 8.0, 20.0, 28.0, 34.0)
FORWARD_FROM = 26.0
FIRST_PACE = 3.6
FORWARD_PACE = 5.4
FORWARD_TICKS = [FORWARD_FROM + 2.9 * n for n in range(12)] + [FORWARD_FROM + 35.0 + 2.1 * n for n in range(16)]


def forward_kernel(
    kind_ref, x_ref, dm_ref, wqkv_ref, wout_ref, wup_ref, wdown_ref, *refs,
):
    small_refs = refs[:NV + 1]
    (
        h1t_ref, qkv_ref, p_ref, attn_ref, rl_ref, x1_ref, dmp_ref, h2t_ref, g_ref, slope_ref, gdown_ref,
        vec_ref, xb_ref, watt_out, wup_out, down_out,
        fa, fb, h1, h2, staged, swap, watt, wup, bqkv, bu, smalls,
        sems_s, sems_r, swap_s, swap_r, small_s, small_r, copy_sem,
    ) = refs[NV + 1:]
    step = pl.program_id(0)
    here = where_am_i()
    z, x, y, c = here
    peers = partners(*here)
    sems = (sems_s, sems_r)

    swaps = [
        remote(staged.at[:, half(i, 1 - c)], swap.at[:, i * HW:(i + 1) * HW], (swap_s, swap_r), i, peers[5])
        for i in range(N_WIDE)
    ]
    items, own = [], []
    for i in range(N_WIDE):
        buf, at = (watt, i) if i < 4 else (wup, i - 4)
        view = lambda zs, xs, ys, buf=buf, at=at: buf.at[zs, xs, ys, :, half(at, c)]
        items.append(Gather(here, sems, i * Gather.COPIES, view, None))
    for i in range(N_DOWN):
        rows, cols = down_rows(i, c), down_cols(i)
        view = lambda zs, xs, ys, rows=rows, cols=cols: down_out.at[zs, xs, ys, rows, cols]
        first = wdown_ref.at[:, :, :, pl.ds((i // 2) * CH, CH), cols]
        items.append(Gather(here, sems, (N_WIDE + i) * Gather.COPIES, view, first))
        own.append(pltpu.make_async_copy(first, view(one(z), one(x), one(y)), copy_sem.at[N_WIDE + i]))
    keeps = []
    for i in range(N_WIDE):
        src, dst, at = (watt, watt_out, i) if i < 4 else (wup, wup_out, i - 4)
        cols = pl.ds(at * D, D)
        keeps.append(pltpu.make_async_copy(
            src.at[:, :, :, :, cols], dst.at[:, :, :, :, cols], copy_sem.at[i]))

    def act(action):
        i, phase = action
        if i >= N_WIDE and phase == 0:
            own[i - N_WIDE].start()
        if i >= N_WIDE and phase == 1:
            own[i - N_WIDE].wait()
        items[i].start(phase)
        if phase == 4 and i < N_WIDE:
            keeps[i].start()

    needed = {1: 4, 2: 8, 3: 11, 4: 12, 5: 16, 6: 20, 7: 24}
    entries = []
    for i in range(1, N_WIDE + N_DOWN):
        for phase in range(5):
            due = FORWARD_PACE * i + FORWARD_LAG[phase] if phase else FIRST_PACE * i
            if i in needed:
                due = min(due, FORWARD_TICKS[needed[i]])
            entries.append((due, (i, phase)))
    early = [a for t, a in sorted(entries, key=lambda e: e[0]) if t < FORWARD_FROM]
    table, late = plan([e for e in entries if e[0] >= FORWARD_FROM], FORWARD_TICKS)

    def tick(slot, could_be):
        for n in could_be:
            if table[n]:
                @pl.when(slot == n)
                def _(n=n):
                    for action in table[n]:
                        act(action)

    @pl.when(step == 0)
    def _():
        say_hello(here)
        for pair in range(6):
            for n in range(3):
                at = pair * 384 + n * 128
                staged[:, at:at + 128] = wqkv_ref[:, n * D + pair * 128:n * D + (pair + 1) * 128].astype(F32)
        staged[:, OUT_AT:UP_AT] = wout_ref[...].astype(F32)
        staged[:, UP_AT:] = wup_ref[...].astype(F32)
        line = smalls.at[z, x, y, c]
        line[...] = jnp.zeros((SR, 128), F32)
        for n, (ref, width) in enumerate(zip(small_refs, VW)):
            line[n:n + 1, 0:width] = ref[...].astype(F32).reshape(1, width)
        await_all()
        swaps[0].start()

        def small_copy(n, src, to):
            return remote(src, src, (small_s, small_r), n, to)

        small_c = small_copy(0, smalls.at[one(z), one(x), one(y), one(c)], peers[5])
        both = smalls.at[one(z), one(x), one(y), TWO]
        small_z = [small_copy(1 + k, both, peers[k]) for k in range(3)]
        small_x = small_copy(4, smalls.at[EVERY, one(x), one(y), TWO], peers[3])
        small_y = small_copy(5, smalls.at[EVERY, TWO, one(y), TWO], peers[4])
        small_c.start()
        for i in range(1, N_WIDE):
            swaps[i].start()

        def take_block(i):
            swaps[i].wait_recv()
            mine_part = staged[:, half(i, c)]
            their_part = swap[:, i * HW:(i + 1) * HW]
            buf, at = (watt, i) if i < 4 else (wup, i - 4)
            lower = jnp.where(c == 0, mine_part, their_part)
            upper = jnp.where(c == 0, their_part, mine_part)
            buf[z, x, y, :, half(at, c)] = jnp.concatenate([lower, upper], 0).astype(BF)

        waiting = list(early)

        def act_some(count):
            for _n in range(min(count, len(waiting))):
                act(waiting.pop(0))

        take_block(0)
        items[0].start(0)
        small_c.wait_recv()
        for copy in small_z:
            copy.start()
        for i in range(1, N_WIDE):
            take_block(i)
        rows_in(x_ref, 0, x1_ref, xb_ref)
        for copy in small_z:
            copy.wait_recv()
        small_x.start()
        act_some(1)
        items[0].start(1)
        rows_in(x_ref, 1, x1_ref, xb_ref)
        small_x.wait_recv()
        small_y.start()
        act_some(1)
        items[0].start(2)
        act_some(1)
        for row in range(2):
            rows_in(dm_ref, row, dmp_ref)
        items[0].start(3)
        small_y.wait_recv()
        src = lax.broadcasted_iota(jnp.int32, (128, D), 0)
        dst = lax.broadcasted_iota(jnp.int32, (128, D), 1)
        spread_short = jnp.where(lax.rem(dst, 24) == src, 1.0, 0.0).astype(BF)
        spread_long = jnp.where(lax.rem(dst, 96) == src, 1.0, 0.0).astype(BF)
        col = lax.broadcasted_iota(jnp.int32, (8, D), 1)
        vec_ref[...] = jnp.zeros_like(vec_ref)

        @pl.loop(0, NZ)
        def _(zi):
            pieces = smalls[zi].reshape(8 * SR, 128).astype(BF)
            short, long = mm(pieces, spread_short), mm(pieces, spread_long)
            for k in range(8):
                at = SR * k
                part = jnp.where(lax.div(col, 24) == zi * 8 + k, short[at:at + NV], 0.0)
                more = jnp.where(lax.div(col, 96) == k, long[at + NV:at + SR], 0.0)
                vectors, hidden_bias = (part, more) if k == 0 else (vectors + part, hidden_bias + more)
            vec_ref[...] += vectors
            bu[zi] = hidden_bias
        for pair in range(6):
            n, at = pair // 2, (pair % 2) * 384
            bqkv[n, :, at:at + 128] = vec_ref[BQ:BQ + 1, pair * 128:(pair + 1) * 128]
            bqkv[n, :, at + 128:at + 256] = jnp.zeros((1, 128), F32)
            bqkv[n, :, at + 256:at + 384] = vec_ref[BV:BV + 1, pair * 128:(pair + 1) * 128]
        act_some(2)

        @pl.loop(0, T // MB)
        def _(i):
            rows = rows_of(i)
            n1, _s = norm_parts(x1_ref[rows, :])
            h1[rows, :] = (n1 * vec_ref[G1:G1 + 1, :] + vec_ref[B1:B1 + 1, :]).astype(BF)
        for row in range(2):
            slot = lax.broadcasted_iota(jnp.int32, (S, 128), 0)
            lane = lax.broadcasted_iota(jnp.int32, (S, 128), 1)
            packed = jnp.where(slot < HALF, 0, jnp.where(slot < 2 * HALF, 1, 2))
            seg = jnp.where(kind_ref[row] == 1, packed, 0)
            fa[row] = jnp.where((lane < 3) & (seg == lane), -1e30, 0.0).astype(BF)
            fb[row] = jnp.where((lane < 3) & ((seg != lane) | (slot >= SEQ)), 1.0, 0.0).astype(BF)
        act_some(len(waiting))
        transpose_into(h1t_ref, h1)
        rl_ref[...] = jnp.zeros_like(rl_ref)
        act((0, 4))
        for copy in (small_c, *small_z, small_x, small_y, *swaps):
            copy.wait_send()

    @pl.when(step < N_ATT)
    def _():
        hq, r = lax.div(step, 2), lax.rem(step, 2)
        tick(2 * step, range(0, 12, 2))

        @pl.when(r == 0)
        def _():
            @pl.loop(0, 2)
            def _(i):
                rows = row_of(i)
                w = watt[:, :, :, :, pl.ds(pl.multiple_of(hq * GW, 128), GW)].reshape(D, GW)
                qkv_ref[rows, :] = (mm(h1[rows, :], w) + bqkv[hq]).astype(BF)

        rows = pl.ds(pl.multiple_of(r * S, 16), S)
        feat_q, feat_k = fa[r], fb[r]
        ones = jnp.ones((S, 128), BF)
        scale = math.log2(math.e) / math.sqrt(HD)
        for j in range(HG // 2):
            if j:
                tick(2 * step + 1, range(1, 12, 2))
            at = j * 384
            qp, kp, vp = (qkv_ref[rows, at + 128 * n: at + 128 * (n + 1)] for n in range(3))
            kcat = jnp.concatenate([kp, feat_k], 1)
            total = None
            for e in range(2):
                keep = head_lanes((S, 128), e)
                qcat = jnp.concatenate([jnp.where(keep, qp, jnp.zeros_like(qp)), feat_q], 1)
                s = mm(qcat, kcat, NT)
                m = jnp.max(s, -1, keepdims=True)
                pb = jnp.exp2((s - m) * scale).astype(BF)
                p_ref[0, 2 * j + e] = pb
                vcat = jnp.concatenate([jnp.where(keep, vp, jnp.zeros_like(vp)), ones], 1)
                o = mm(pb, vcat)
                rl = 1.0 / o[:, 128:]
                part = o[:, :128] * rl
                total = part if total is None else total + part
                spot = lax.broadcasted_iota(jnp.int32, (S, 128), 1) == hq * HG + 2 * j + e
                rl_ref[rows, :] = jnp.where(spot, rl, rl_ref[rows, :])
            out = pl.ds(pl.multiple_of(hq * QW + j * 128, 128), 128)
            attn_ref[rows, out] = total.astype(BF)

    @pl.when(step == N_ATT - 1)
    def _():
        @pl.loop(0, T // MB)
        def _(i):
            rows = rows_of(i)
            wo = watt[:, :, :, :, OUT_AT:UP_AT].reshape(D, D)
            x1 = x1_ref[rows, :] + mm(attn_ref[rows, :], wo) + vec_ref[BO:BO + 1, :]
            x1_ref[rows, :] = x1
            n2, _s = norm_parts(x1)
            h2[rows, :] = (n2 * vec_ref[G2:G2 + 1, :] + vec_ref[B2:B2 + 1, :]).astype(BF)
        transpose_into(h2t_ref, h2)

    @pl.when(step >= N_ATT)
    def _():
        part = step - N_ATT

        @pl.loop(0, 2)
        def _(i):
            tick(12 + 4 * part + 2 * i, range(12, len(FORWARD_TICKS), 2))
            tick(12 + 4 * part + 2 * i + 1, range(13, len(FORWARD_TICKS), 2))
            rows = row_of(i)
            w = wup[:, :, :, :, pl.ds(pl.multiple_of(part * D, 128), D)].reshape(D, D)
            g, slope = gelu_both(mm(h2[rows, :], w) + bu[part, 0:1, :])
            g_ref[rows, :] = g.astype(BF)
            slope_ref[rows, :] = slope.astype(BF)

        @pl.loop(0, 2)
        def _(t):
            cols = pl.ds(pl.multiple_of(t * 384, 128), 384)
            gdown_ref[cols, :] = mm(g_ref[:, cols], dmp_ref[...], TN).astype(BF)

    @pl.when(step == N_ATT + N_UP - 1)
    def _():
        for action in late:
            act(action)
        for item in items:
            item.drain()
        for copy in keeps:
            copy.wait()


def forward(kind, x, dm, wqkv, wout, wup, wdown, smalls):
    n = N_WIDE + N_DOWN
    att = lambda s: jnp.minimum(s, N_ATT - 1)
    ff = lambda s: jnp.maximum(s - N_ATT, 0)
    shape = jax.ShapeDtypeStruct
    return pl.pallas_call(
        forward_kernel,
        grid=(N_ATT + N_UP,),
        in_specs=[
            pl.BlockSpec(memory_space=pltpu.SMEM), fixed((SEQ, 2, D)), fixed((SEQ, 2, D)),
            fixed((24, 3 * D)), fixed((24, D)), fixed((24, FF)), fixed((1, 1, 1, 96, D)),
            *[pl.BlockSpec((w,), lambda s: (0,), pipeline_mode=pl.Buffered(1)) for w in VW],
        ],
        out_specs=[
            fixed((D, T)), pl.BlockSpec((T, GW), lambda s: (0, att(s) // 2)),
            pl.BlockSpec((1, HG, S, S), lambda s: (att(s) % 2, att(s) // 2, 0, 0)),
            fixed((T, D)), fixed((T, 128)), fixed((T, D)), fixed((T, D)), fixed((D, T)),
            pl.BlockSpec((T, D), lambda s: (0, ff(s))), pl.BlockSpec((T, D), lambda s: (0, ff(s))),
            pl.BlockSpec((D, D), lambda s: (ff(s), 0)),
            fixed((NV, D)), fixed((T, D)), hbm(), hbm(), hbm(),
        ],
        out_shape=[
            shape((D, T), BF), shape((T, 3 * D), BF), shape((2, D // HD, S, S), BF),
            shape((T, D), BF), shape((T, 128), F32), shape((T, D), F32), shape((T, D), BF), shape((D, T), BF),
            shape((T, FF), BF), shape((T, FF), BF), shape((FF, D), BF), shape((NV, D), F32), shape((T, D), BF),
            shape((NZ, 2, 2, CH, UP_AT), BF), shape((NZ, 2, 2, CH, FF), BF), shape((NZ, 2, 2, 4 * CH, D), BF),
        ],
        scratch_shapes=[
            pltpu.VMEM((2, S, 128), BF), pltpu.VMEM((2, S, 128), BF), pltpu.VMEM((T, D), BF), pltpu.VMEM((T, D), BF),
            pltpu.VMEM((24, AW), F32), pltpu.VMEM((24, AW // 2), F32),
            pltpu.VMEM((NZ, 2, 2, CH, UP_AT), BF), pltpu.VMEM((NZ, 2, 2, CH, FF), BF),
            pltpu.VMEM((3, 1, GW), F32), pltpu.VMEM((N_UP, 8, D), F32), pltpu.VMEM((NZ, 2, 2, 2, SR, 128), F32),
            *dma_sems(n * Gather.COPIES, n * Gather.COPIES, N_WIDE, N_WIDE, 6, 6, n),
        ],
        compiler_params=pltpu.CompilerParams(collective_id=0, has_side_effects=True, vmem_limit_bytes=LIMIT),
        name="forward",
    )(kind, x, dm, wqkv, wout, wup, wdown.reshape(1, 1, 1, 96, D), *smalls)


BACK_LAG = (0.0, 5.0, 15.0, 23.0, 32.0)
FFN_TICKS = [4.0 + 9.0 * s + t for s in range(4) for t in (0.0, 0.1, 2.8, 2.9, 5.7, 7.3)]


def ffn_back_kernel(
    x1_ref, dm_ref, g_ref, slope_ref, wu_ref, wd_ref, h2t_ref, vec_ref, gdown_ref,
    y_ref, dx1_ref, gup_ref, sums_ref, odown_ref,
    yacc, dacc, dus, mine, acc, via, last, zs, sems_s, sems_r, own_sem,
):
    step = pl.program_id(0)
    here = where_am_i()
    z, x, y, c = here
    items, own = [], []
    for i in range(N_DOWN):
        rows, cols = down_rows(i, c), down_cols(i)
        own.append(pltpu.make_async_copy(gdown_ref.at[:, :, :, rows, cols], mine.at[i], own_sem.at[i]))
        items.append(Scatter(
            here, (sems_s, sems_r), i * Scatter.COPIES, gdown_ref.at[EVERY, TWO, TWO, down_rows(i, 1 - c), cols],
            lambda a, b, d, i=i: mine[i, a, b, d], acc.at[i], via.at[i], last.at[i], zs.at[i],
        ))
    entries = [
        (5.0 + PACE * i + lag, (i, phase)) for i in range(N_DOWN) for phase, lag in enumerate(BACK_LAG) if (i, phase) != (0, 0)
    ]
    table, late = plan(entries, FFN_TICKS)

    def act(action):
        i, phase = action
        if phase == 1:
            own[i].wait()
        if phase == 4:
            odown_ref[pl.ds((i // 2) * CH, CH), down_cols(i)] = items[i].total()
        else:
            items[i].start(phase)

    def tick(slot):
        for n, todo in table.items():
            if todo:
                @pl.when(slot == n)
                def _(todo=todo):
                    for action in todo:
                        act(action)

    @pl.when(step == 0)
    def _():
        say_hello(here)
        for copy in own:
            copy.start()

        @pl.loop(0, T // MB)
        def _(i):
            rows = rows_of(i)
            yacc[rows, :] = x1_ref[rows, :] + vec_ref[BD:BD + 1, :]
            dacc[rows, :] = jnp.zeros((MB, D), F32)
        sums_ref[...] = jnp.zeros_like(sums_ref)
        sums_ref[2:3, :] = jnp.sum(dm_ref[...].astype(F32), 0, keepdims=True)

    @pl.loop(0, 2)
    def _(i):
        @pl.when((step == 0) & (i == 1))
        def _():
            await_all()
            act((0, 0))

        tick(6 * step + 2 * i)
        tick(6 * step + 2 * i + 1)
        rows = row_of(i)
        g = g_ref[rows, :]
        yacc[rows, :] += mm(g, wd_ref[...])
        du = (mm(dm_ref[rows, :], wd_ref[...], NT) * slope_ref[rows, :].astype(F32)).astype(BF)
        dus[rows, :] = du
        sums_ref[pl.ds(3 + step, 1), :] += jnp.sum(du.astype(F32), 0, keepdims=True)
        dacc[rows, :] += mm(du, wu_ref[...], NT)

    @pl.loop(0, 2)
    def _(t):
        tick(6 * step + 4 + t)
        rows = pl.ds(pl.multiple_of(t * 384, 128), 384)
        gup_ref[rows, :] = mm(h2t_ref[rows, :], dus[...]).astype(BF)

    @pl.when(step == N_UP - 1)
    def _():
        @pl.loop(0, T // MB)
        def _(i):
            rows = rows_of(i)
            n2, s2 = norm_parts(x1_ref[rows, :])
            dh = dacc[rows, :]
            sums_ref[0:1, :] += jnp.sum(dh * n2, 0, keepdims=True)
            sums_ref[1:2, :] += jnp.sum(dh, 0, keepdims=True)
            dx1_ref[rows, :] = dm_ref[rows, :].astype(F32) + norm_pull(dh, n2, s2, vec_ref[G2:G2 + 1, :])
            y_ref[rows, :] = yacc[rows, :].astype(BF)
        for action in late:
            act(action)
        for item in items:
            item.drain()


def ffn_back(x1, dm, g, slope, wup, down, h2t, vec, gdown):
    shape = jax.ShapeDtypeStruct
    col = pl.BlockSpec((T, D), lambda s: (0, s))
    return pl.pallas_call(
        ffn_back_kernel,
        grid=(N_UP,),
        in_specs=[
            fixed((T, D)), fixed((T, D)), col, col,
            pl.BlockSpec((D, D), lambda s: (0, s)), pl.BlockSpec((D, D), lambda s: (s, 0)),
            fixed((D, T)), fixed((NV, D)), hbm(),
        ],
        out_specs=[
            fixed((T, D)), fixed((T, D)), pl.BlockSpec((D, D), lambda s: (0, s)), fixed((8, D)), fixed((96, D)),
        ],
        out_shape=[
            shape((T, D), BF), shape((T, D), F32), shape((D, FF), BF), shape((8, D), F32), shape((96, D), F32),
        ],
        scratch_shapes=[
            pltpu.VMEM((T, D), F32), pltpu.VMEM((T, D), F32), pltpu.VMEM((T, D), BF),
            pltpu.VMEM((N_DOWN, NZ, 2, 2, CH, HW), BF), *scatter_bufs(N_DOWN, HW),
            *dma_sems(N_DOWN * 7, N_DOWN * 7, N_DOWN),
        ],
        compiler_params=pltpu.CompilerParams(collective_id=1, has_side_effects=True, vmem_limit_bytes=LIMIT),
        name="feed_forward_back",
    )(x1, dm, g, slope, wup, down, h2t, vec, gdown.reshape(NZ, 2, 2, 4 * CH, D))


BACK_TICKS = [2.0 + 4.8 * n for n in range(12)]
N_BACK = N_UP + 4
END_LAG = (0.0, 4.0, 9.0, 14.0, 19.0)


def attn_back_kernel(
    xb_ref, yb_ref, dx1_ref, h1t_ref, qkv_ref, p_ref, attn_ref, rl_ref, wo_ref, wqkv_ref, vec_ref, sums_ref, gup_ref,
    out_ref, gx_ref, oqkv_ref, oout_ref, oup_ref, *refs,
):
    small_outs = refs[:NV + 1]
    (
        da, dos, dqkv, dh1, gqkv, gout, mine, acc, via, last, zs, done, landed, small,
        sems_s, sems_r, fin_s, fin_r, small_s, small_r, own_sem,
    ) = refs[NV + 1:]
    step = pl.program_id(0)
    hq, r = lax.div(step, 2), lax.rem(step, 2)
    here = where_am_i()
    z, x, y, c = here
    peers = partners(*here)
    items, own = [], []
    for n in range(N_BACK):
        if n < N_UP:
            theirs = gup_ref.at[EVERY, TWO, TWO, :, half(n, 1 - c)]
            own.append(pltpu.make_async_copy(gup_ref.at[:, :, :, :, half(n, c)], mine.at[n], own_sem.at[n]))
            get = lambda a, b, d, n=n: mine[n, a, b, d]
        elif n == N_UP:
            theirs = gout.at[EVERY, TWO, TWO, :, half(0, 1 - c)]
            get = lambda a, b, d: gout[a, b, d, :, half(0, c)]
        else:
            i = n - N_UP - 1
            theirs = gqkv.at[i, EVERY, TWO, TWO, :, half(0, 1 - c)]
            get = lambda a, b, d, i=i: gqkv[i, a, b, d, :, half(0, c)]
        items.append(Scatter(
            here, (sems_s, sems_r), n * Scatter.COPIES, theirs, get, acc.at[n], via.at[n], last.at[n], zs.at[n]))

    def final(n):
        theirs = pl.ds(pl.multiple_of((1 - c) * 24, 8), 24)
        return remote(done.at[n, theirs], landed.at[n], (fin_s, fin_r), n, peers[5])

    def put(n, core, value):
        if n > N_UP:
            for b in range(3):
                cols = pl.ds(pl.multiple_of(b * D + (n - N_UP - 1) * QW + core * 128, 128), 128)
                oqkv_ref[:, cols] = value[:, b * 128:(b + 1) * 128]
        elif n == N_UP:
            oout_ref[:, half(0, core)] = value
        else:
            oup_ref[:, half(n, core)] = value

    def finish(n):
        done[n] = items[n].total()
        final(n).start()
        put(n, c, done[n, pl.ds(pl.multiple_of(c * 24, 8), 24)])

    def act(action):
        n, phase = action
        if n < N_UP and phase == 1:
            own[n].wait()
        if phase == 4:
            finish(n)
        else:
            items[n].start(phase)

    entries = []
    begin = 0.0
    for n in range(N_BACK):
        if n > N_UP:
            begin = max(begin, BACK_TICKS[0] + 19.2 * (n - N_UP))
        for phase in range(5):
            if n < N_UP or phase > 0:
                lag = BACK_LAG if n < N_BACK - 2 else END_LAG
                entries.append((begin + lag[phase], (n, phase)))
        begin += PACE
    entries.remove((0.0, (0, 0)))
    table, tail = plan(entries, BACK_TICKS)
    final_steps = [a for a in tail if a[0] == N_BACK - 1]
    earlier = [a for a in tail if a[0] != N_BACK - 1]

    def tick(slot, could_be):
        for n in could_be:
            if table[n]:
                @pl.when(slot == n)
                def _(n=n):
                    for action in table[n]:
                        act(action)

    @pl.when(step == 0)
    def _():
        say_hello(here)
        for copy in own:
            copy.start()
        small[0] = jnp.zeros((16, D), F32)
        src = lax.broadcasted_iota(jnp.int32, (128, D), 0)
        dst = lax.broadcasted_iota(jnp.int32, (128, D), 1)
        spread = jnp.where(lax.div(dst, HD) == src, 1.0, 0.0)

        @pl.loop(0, T // MB)
        def _(i):
            rows = rows_of(i)
            d = dx1_ref[rows, :].astype(BF)
            da[rows, :] = d
            rl = lax.dot_general(
                rl_ref[rows, :], spread, NN, precision=lax.Precision.HIGHEST, preferred_element_type=F32)
            small[0, 4:5, :] += jnp.sum(d.astype(F32), 0, keepdims=True)
            dos[rows, :] = (mm(d, wo_ref[...], NT) * rl).astype(BF)
            dh1[rows, :] = jnp.zeros((MB, D), F32)
        @pl.loop(0, 2)
        def _(t):
            part = mm(attn_ref[:, pl.ds(pl.multiple_of(t * 384, 128), 384)], da[...], TN)
            gout[pl.ds(2 * t, 2)] = part.astype(BF).reshape(2, 2, 2, CH, D)

        await_all()
        act((0, 0))
        items[N_UP].start(0)

    tick(2 * step, range(0, 12, 2))
    rows = pl.ds(pl.multiple_of(r * S, 16), S)
    scale = 1.0 / math.sqrt(HD)
    for j in range(HG // 2):
        if j:
            tick(2 * step + 1, range(1, 12, 2))
        at = j * 384
        qp, kp, vp = (qkv_ref[rows, at + 128 * n: at + 128 * (n + 1)] for n in range(3))
        lanes = pl.ds(pl.multiple_of(hq * QW + j * 128, 128), 128)
        do = dos[rows, lanes]
        prod = do.astype(F32) * attn_ref[rows, lanes].astype(F32)
        dq = dk = dv = None
        for e in range(2):
            keep = head_lanes((S, 128), e)
            zero = jnp.zeros_like(qp)
            doe = jnp.where(keep, do, zero)
            dot = jnp.sum(jnp.where(keep, prod, 0.0), -1, keepdims=True)
            p = p_ref[0, 2 * j + e]
            ds = (p.astype(F32) * (mm(doe, vp, NT) - dot)).astype(BF)
            a_, b_, c_ = mm(ds, jnp.where(keep, kp, zero)), mm(ds, jnp.where(keep, qp, zero), TN), mm(p, doe, TN)
            dq, dk, dv = (a_, b_, c_) if dq is None else (dq + a_, dk + b_, dv + c_)
        for n, part in enumerate((dq * scale, dk * scale, dv)):
            dqkv[rows, at + 128 * n:at + 128 * (n + 1)] = part.astype(BF)

    @pl.when(r == 1)
    def _():
        sums = jnp.sum(dqkv[...].astype(F32), 0, keepdims=True)
        for j in range(2):
            cols = pl.ds(pl.multiple_of(hq * QW + j * 128, 128), 128)
            small[0, 2:3, cols] = sums[:, j * 384:j * 384 + 128]
            small[0, 3:4, cols] = sums[:, j * 384 + 256:j * 384 + 384]
        @pl.loop(0, 2)
        def _(t):
            part = mm(h1t_ref[pl.ds(pl.multiple_of(t * 384, 16), 384), :], dqkv[...])
            gqkv[hq, pl.ds(2 * t, 2)] = part.astype(BF).reshape(2, 2, 2, CH, GW)

        for i in range(3):
            @pl.when(hq == i)
            def _(i=i):
                items[N_UP + 1 + i].start(0)

        @pl.loop(0, 2)
        def _(i):
            rr = row_of(i)
            dh1[rr, :] += mm(dqkv[rr, :], wqkv_ref[...], NT)

    @pl.when(step == N_ATT - 1)
    def _():
        rest = final_steps[1:]

        @pl.loop(0, T // MB)
        def _(i):
            @pl.when(i == 0)
            def _():
                for action in earlier[:-1]:
                    act(action)

            @pl.when(i == 1)
            def _():
                act(final_steps[0])

            @pl.when(i == 3)
            def _():
                for action in earlier[-1:]:
                    act(action)
            rr = rows_of(i)
            dh = dh1[rr, :]
            n1, s1 = norm_parts(xb_ref[rr, :].astype(F32))
            small[0, 0:1, :] += jnp.sum(dh * n1, 0, keepdims=True)
            small[0, 1:2, :] += jnp.sum(dh, 0, keepdims=True)
            da[rr, :] = (dx1_ref[rr, :] + norm_pull(dh, n1, s1, vec_ref[G1:G1 + 1, :])).astype(BF)
        small[0, 5:12, :] = sums_ref[0:7, :]
        copies = []

        def send_small(n, src, dst, to):
            copy = remote(small.at[src], small.at[dst], (small_s, small_r), n, to)
            copy.start()
            copies.append(copy)

        send_small(0, 0, 1, peers[5])
        hops = [(1, 2, 3, peers[3]), (2, 4, 5, peers[4])]
        level = 0
        while rest or level < 4:
            if rest:
                act(rest.pop(0))
            if level == 0:
                for row in range(2):
                    rows_out(da, gx_ref, row)
            if level == 1:
                for row in range(2):
                    rows_out(yb_ref, out_ref, row)
            if level < 2:
                copies[level].wait_recv()
                small[2 * level + 2] = small[2 * level] + small[2 * level + 1]
                send_small(*hops[level])
            elif level == 2:
                copies[2].wait_recv()
                small[6] = small[4] + small[5]
                for k in range(3):
                    send_small(3 + k, 6, 7 + k, peers[k])
            elif level == 3:
                for k in range(3):
                    copies[3 + k].wait_recv()
                total = small[6] + small[7] + small[8] + small[9]
                me = lax.axis_index("dp") * lax.axis_size("fsdp") + lax.axis_index("fsdp")
                src = lax.broadcasted_iota(jnp.int32, (D, 128), 0)
                dst = lax.broadcasted_iota(jnp.int32, (D, 128), 1)

                def pick(lines, width, at):
                    chosen = jnp.where((src == at + dst) & (dst < width), 1.0, 0.0)
                    return lax.dot_general(
                        lines, chosen, NN, precision=lax.Precision.HIGHEST, preferred_element_type=F32)

                mine_of = pick(total[:8], 24, me * 24)
                for n in range(NV):
                    small_outs[n][...] = mine_of[n, :24]
                row = lax.broadcasted_iota(jnp.int32, (8, D), 0)
                longest = jnp.sum(jnp.where(row == lax.div(me, 8), total[8:16], 0.0), 0, keepdims=True)
                small_outs[NV][...] = pick(jnp.broadcast_to(longest, (8, D)), 96, lax.rem(me, 8) * 96)[0, :96]
            level += 1
        for n in range(N_BACK):
            copy = final(n)
            copy.wait_recv()
            put(n, 1 - c, landed[n])
            copy.wait_send()
            items[n].drain()
        for copy in copies:
            copy.wait_send()


def attn_back(x, yb, dx1, h1t, qkv, p, attn, rl, watt, vec, sums, gup):
    shape = jax.ShapeDtypeStruct
    n_fin = N_BACK
    return pl.pallas_call(
        attn_back_kernel,
        grid=(N_ATT,),
        in_specs=[
            fixed((T, D)), fixed((T, D)), fixed((T, D)), fixed((D, T)), pl.BlockSpec((T, GW), lambda s: (0, s // 2)),
            pl.BlockSpec((1, HG, S, S), lambda s: (s % 2, s // 2, 0, 0)), fixed((T, D)), fixed((T, 128)),
            pl.BlockSpec((D, D), lambda s: (0, 3), pipeline_mode=pl.Buffered(1)),
            pl.BlockSpec((D, GW), lambda s: (0, s // 2)), fixed((NV, D)), fixed((8, D)), hbm(),
        ],
        out_specs=[
            fixed((SEQ, 2, D)), fixed((SEQ, 2, D)), fixed((24, 3 * D)), fixed((24, D)), fixed((24, FF)),
            *[pl.BlockSpec((w,), lambda s: (0,), pipeline_mode=pl.Buffered(1)) for w in VW],
        ],
        out_shape=[
            shape((SEQ, 2, D), BF), shape((SEQ, 2, D), BF), shape((24, 3 * D), F32), shape((24, D), F32),
            shape((24, FF), F32), *[shape((w,), F32) for w in VW],
        ],
        scratch_shapes=[
            pltpu.VMEM((T, D), BF), pltpu.VMEM((T, D), BF), pltpu.VMEM((T, GW), BF), pltpu.VMEM((T, D), F32),
            pltpu.VMEM((3, NZ, 2, 2, CH, GW), BF), pltpu.VMEM((NZ, 2, 2, CH, D), BF),
            pltpu.VMEM((N_UP, NZ, 2, 2, CH, HW), BF), *scatter_bufs(N_BACK, HW),
            pltpu.VMEM((N_BACK, CH, HW), F32), pltpu.VMEM((N_BACK, 24, HW), F32), pltpu.VMEM((10, 16, D), F32),
            *dma_sems(N_BACK * 7, N_BACK * 7, n_fin, n_fin, 6, 6, N_UP),
        ],
        compiler_params=pltpu.CompilerParams(collective_id=2, has_side_effects=True, vmem_limit_bytes=LIMIT),
        name="attention_back",
    )(x, yb, dx1, h1t, qkv, p, attn, rl, watt, watt, vec, sums, gup.reshape(NZ, 2, 2, CH, FF))


def hand_over_kernel(*refs):
    n = len(refs) // 2
    for i in range(n):
        refs[n + i][...] = refs[i][...]


def hand_over(values):
    return pl.pallas_call(
        hand_over_kernel,
        in_specs=[vmem()] * len(values),
        out_specs=[vmem()] * len(values),
        out_shape=[jax.ShapeDtypeStruct(v.shape, v.dtype) for v in values],
        compiler_params=pltpu.CompilerParams(vmem_limit_bytes=LIMIT),
        name="results",
    )(*values)


def by_pair(v):
    return v.reshape(v.shape[0], 3, 6, 128).transpose(0, 2, 1, 3).reshape(v.shape[0], 3 * D)


def by_kind(v):
    return v.reshape(v.shape[0], 6, 3, 128).transpose(0, 2, 1, 3).reshape(v.shape[0], 3 * D)


def with_own_copies(inputs, row_kind, w_qkv, w_out, w_up, w_down, vectors, b_up, out_grad):
    x, dm = inputs.transpose(1, 0, 2), out_grad.transpose(1, 0, 2)
    h1t, qkv, p, attn, rl, x1, dmp, h2t, g, slope, gdown, vec, xb, watt, wup, down = forward(
        row_kind, x, dm, w_qkv, w_out, w_up, w_down, (*vectors, b_up))
    yb, dx1, gup, sums, gdown = ffn_back(
        x1, dmp, g, slope, wup.reshape(D, FF), down.reshape(FF, D), h2t, vec, gdown)
    results = attn_back(xb, yb, dx1, h1t, qkv, p, attn, rl, watt.reshape(D, UP_AT), vec, sums, gup)
    out, gx, gqkv, gout, gup, gdown, *small = hand_over((*results[:5], gdown, *results[5:]))
    return out.transpose(1, 0, 2), gx.transpose(1, 0, 2), gqkv, gout, gup, gdown, small[:NV], small[NV]


def with_collectives(inputs, row_kind, w_qkv, w_out, w_up, w_down, vectors, b_up, out_grad):
    axes = ("dp", "fsdp")
    get = lambda v: lax.all_gather(v, axes, axis=0, tiled=True)
    wide = jnp.concatenate([by_pair(get(w_qkv)), get(w_out), get(w_up)], 1)
    down = get(w_down)
    full = [get(v).astype(F32) for v in vectors]
    vec = jnp.stack(full)
    bu = get(b_up).astype(F32)[None]
    bqkv = by_pair(jnp.concatenate([full[BQ], jnp.zeros_like(full[BQ]), full[BV]])[None])
    h1, qkv, p, attn, rl, x1 = attn_fwd(row_kind, inputs, wide, bqkv, vec)
    outputs, dx1, gup, gdown, gbu, gg2, gb2, gbd = ffn(x1, out_grad, wide, down, bu, vec)
    input_grad, gqkv, gout, gbqkv, gbo, gg1, gb1 = attn_bwd(inputs, dx1, h1, qkv, p, attn, rl, wide, vec)
    gbqkv = by_kind(gbqkv)
    small = [gg1, gb1, gbqkv[:, :D], gbqkv[:, 2 * D:], gbo, gg2, gb2, gbd]
    give = lambda v: lax.psum_scatter(v.astype(F32), axes, scatter_dimension=0, tiled=True)
    return (
        outputs, input_grad, give(by_kind(gqkv)), give(gout), give(gup), give(gdown),
        [give(v[0]) for v in small], give(gbu[0]),
    )


def on_device(
    copies, inputs, row_kind, ln1_gain, ln1_bias, w_qkv, b_query, b_value, w_out, b_out, ln2_gain, ln2_bias,
    w_up, b_up, w_down, b_down, out_grad,
):
    vectors = (ln1_gain, ln1_bias, b_query, b_value, b_out, ln2_gain, ln2_bias, b_down)
    run = with_own_copies if copies else with_collectives
    outputs, input_grad, gqkv, gout, gup, gdown, small, gbu = run(
        inputs, row_kind, w_qkv, w_out, w_up, w_down, vectors, b_up, out_grad)
    gg1, gb1, gbq, gbv, gbo, gg2, gb2, gbd = small
    return outputs, input_grad, gg1, gb1, gqkv, gbq, gbv, gout, gbo, gg2, gb2, gup, gbu, gdown, gbd


def solution(mesh):
    both = ("dp", "fsdp")
    row = P(both)
    mat = P(both, None)
    act = P(both, None, None)
    in_specs = (act, row, row, row, mat, row, row, mat, row, row, row, mat, row, mat, row, act)
    out_specs = (act, act, row, row, mat, row, row, mat, row, row, row, mat, row, mat, row)
    copies = mesh.shape["dp"] == 2 * NZ and mesh.shape["fsdp"] == 4
    return jax.shard_map(
        functools.partial(on_device, copies), mesh=mesh, in_specs=in_specs, out_specs=out_specs, check_vma=False
    )
```

profile of v0, /device:TPU:0, one launch (start us, length us, event | category | flops | bytes accessed | tf_op | source)
XLA Modules:
  0.0 240.5 jit_solution(9331559564302416372)
XLA Ops:
  0.7 103.6 %forward.1 = (bf16[768,1088]{1,0:T(8,128)(2,1)}, bf16[1088,2304]{1,0:T(8,128)(2,1)}, bf16[2,12,544,544]{3,2,1,0:T(8,128)(2,1)}, bf16[1088,768]{1,0:T(8,128)(2,1)...) custom-call(s32[2]{0:T(128)} %kind_ref.1, ...), custom_call_target="tpu_custom_call" | custom-call | tf_op jit(solution)/shard_map/forward/pallas_call | solution.py:884
  104.2 49.1 %feed_forward_back.1 = (bf16[1088,768]{1,0:T(8,128)(2,1)}, f32[1088,768]{1,0:T(8,128)}, bf16[768,3072]{1,0:T(8,128)(2,1)}, f32[8,768]{1,0:T(8,128)}, f32[96,768]{1,0:T(8,128)}) custom-call(f32[1088,768]{1,0:T(8,128)} %get-tuple-element.66.x1_ref, bf16[1088,768]{1,0:T(8,128)(2,1)} %get-tuple-element.67.dm_ref, bf16[1088,3072]{1,0:T(8,128)(2,1)} %get-tuple-element.68.g_ref, ...), custom_call_target="tpu_custom_call" | custom-call | tf_op jit(solution)/shard_map/feed_forward_back/pallas_call | solution.py:1017
  153.4 82.6 %attention_back.1 = (bf16[529,2,768]{2,1,0:T(2,128)(2,1)}, bf16[529,2,768]{2,1,0:T(2,128)(2,1)}, f32[24,2304]{1,0:T(8,128)}, f32[24,768]{1,0:T(8,128)}, f32[24,3...) custom-call(bf16[1088,768]{1,0:T(8,128)(2,1)} %get-tuple-element.65., ...), custom_call_target="tpu_custom_call" | custom-call | tf_op jit(solution)/shard_map/attention_back/pallas_call | solution.py:1289
  235.9 4.4 %results.1 = (bf16[529,2,768]{2,1,0:T(2,128)(2,1)}, bf16[529,2,768]{2,1,0:T(2,128)(2,1)}, f32[24,2304]{1,0:T(8,128)}, f32[24,768]{1,0:T(8,128)}, f32[24,3072]{1,...) custom-call(bf16[529,2,768]{2,1,0:T(2,128)(2,1)} %get-tuple-element., ...), custom_call_target="tpu_custom_call" | custom-call | tf_op jit(solution)/shard_map/results/pallas_call | solution.py:1325
where the time goes:
time: 241 us; the launch traced here: 240 us
  Pallas kernels  240 us (100%)
    pallas_call x1, Pallas kernels, forward(): pl.pallas_call(forward_kernel, grid=(N_ATT + N_UP,), in_specs=[pl.BlockSp...  104 us
    pallas_call x1, Pallas kernels, attn_back(): pl.pallas_call(attn_back_kernel, grid=(N_ATT,), in_specs=[fixed((T, D)),...  82.6 us
    pallas_call x1, Pallas kernels, ffn_back(): pl.pallas_call(ffn_back_kernel, grid=(N_UP,), in_specs=[fixed((T, D)), fi...  49.1 us

commit v1 on v0

--- a/solution.py
+++ b/solution.py
@@ -622,8 +622,9 @@
 ):
     small_refs = refs[:NV + 1]
     (
-        h1t_ref, qkv_ref, p_ref, attn_ref, rl_ref, x1_ref, dmp_ref, h2t_ref, g_ref, slope_ref, gdown_ref,
-        vec_ref, xb_ref, watt_out, wup_out, down_out,
+        h1t_out, qkv_ref, p_ref, attn_out, rl_out, x1_out, dmp_out, h2t_out, g_ref, slope_ref, gdown_ref,
+        vec_ref, xb_out, watt_out, wup_out, down_out,
+        h1t_ref, attn_ref, rl_ref, x1_ref, dmp_ref, h2t_ref, xb_ref, out_sem,
         fa, fb, h1, h2, staged, swap, watt, wup, bqkv, bu, smalls,
         sems_s, sems_r, swap_s, swap_r, small_s, small_r, copy_sem,
     ) = refs[NV + 1:]
@@ -654,6 +655,15 @@
         cols = pl.ds(at * D, D)
         keeps.append(pltpu.make_async_copy(
             src.at[:, :, :, :, cols], dst.at[:, :, :, :, cols], copy_sem.at[i]))
+
+    first_out = [
+        pltpu.make_async_copy(a, b, out_sem.at[n])
+        for n, (a, b) in enumerate(((h1t_ref, h1t_out), (dmp_ref, dmp_out), (xb_ref, xb_out)))
+    ]
+    next_out = [
+        pltpu.make_async_copy(a, b, out_sem.at[3 + n])
+        for n, (a, b) in enumerate(((attn_ref, attn_out), (rl_ref, rl_out), (x1_ref, x1_out), (h2t_ref, h2t_out)))
+    ]
 
     def act(action):
         i, phase = action
@@ -789,6 +799,8 @@
             fb[row] = jnp.where((lane < 3) & ((seg != lane) | (slot >= SEQ)), 1.0, 0.0).astype(BF)
         act_some(len(waiting))
         transpose_into(h1t_ref, h1)
+        for copy in first_out:
+            copy.start()
         rl_ref[...] = jnp.zeros_like(rl_ref)
         act((0, 4))
         for copy in (small_c, *small_z, small_x, small_y, *swaps):
@@ -846,6 +858,8 @@
             n2, _s = norm_parts(x1)
             h2[rows, :] = (n2 * vec_ref[G2:G2 + 1, :] + vec_ref[B2:B2 + 1, :]).astype(BF)
         transpose_into(h2t_ref, h2)
+        for copy in next_out:
+            copy.start()
 
     @pl.when(step >= N_ATT)
     def _():
@@ -872,7 +886,7 @@
             act(action)
         for item in items:
             item.drain()
-        for copy in keeps:
+        for copy in (*keeps, *first_out, *next_out):
             copy.wait()
 
 
@@ -890,12 +904,12 @@
             *[pl.BlockSpec((w,), lambda s: (0,), pipeline_mode=pl.Buffered(1)) for w in VW],
         ],
         out_specs=[
-            fixed((D, T)), pl.BlockSpec((T, GW), lambda s: (0, att(s) // 2)),
+            hbm(), pl.BlockSpec((T, GW), lambda s: (0, att(s) // 2)),
             pl.BlockSpec((1, HG, S, S), lambda s: (att(s) % 2, att(s) // 2, 0, 0)),
-            fixed((T, D)), fixed((T, 128)), fixed((T, D)), fixed((T, D)), fixed((D, T)),
+            hbm(), hbm(), hbm(), hbm(), hbm(),
             pl.BlockSpec((T, D), lambda s: (0, ff(s))), pl.BlockSpec((T, D), lambda s: (0, ff(s))),
             pl.BlockSpec((D, D), lambda s: (ff(s), 0)),
-            fixed((NV, D)), fixed((T, D)), hbm(), hbm(), hbm(),
+            fixed((NV, D)), hbm(), hbm(), hbm(), hbm(),
         ],
         out_shape=[
             shape((D, T), BF), shape((T, 3 * D), BF), shape((2, D // HD, S, S), BF),
@@ -904,6 +918,8 @@
             shape((NZ, 2, 2, CH, UP_AT), BF), shape((NZ, 2, 2, CH, FF), BF), shape((NZ, 2, 2, 4 * CH, D), BF),
         ],
         scratch_shapes=[
+            pltpu.VMEM((D, T), BF), pltpu.VMEM((T, D), BF), pltpu.VMEM((T, 128), F32), pltpu.VMEM((T, D), F32),
+            pltpu.VMEM((T, D), BF), pltpu.VMEM((D, T), BF), pltpu.VMEM((T, D), BF), *dma_sems(7),
             pltpu.VMEM((2, S, 128), BF), pltpu.VMEM((2, S, 128), BF), pltpu.VMEM((T, D), BF), pltpu.VMEM((T, D), BF),
             pltpu.VMEM((24, AW), F32), pltpu.VMEM((24, AW // 2), F32),
             pltpu.VMEM((NZ, 2, 2, CH, UP_AT), BF), pltpu.VMEM((NZ, 2, 2, CH, FF), BF),
@@ -916,13 +932,15 @@
 
 
 BACK_LAG = (0.0, 5.0, 15.0, 23.0, 32.0)
+FFN_LAG = (0.0, 4.0, 13.0, 20.0, 27.0)
+FFN_PACE = 4.0
 FFN_TICKS = [4.0 + 9.0 * s + t for s in range(4) for t in (0.0, 0.1, 2.8, 2.9, 5.7, 7.3)]
 
 
 def ffn_back_kernel(
-    x1_ref, dm_ref, g_ref, slope_ref, wu_ref, wd_ref, h2t_ref, vec_ref, gdown_ref,
-    y_ref, dx1_ref, gup_ref, sums_ref, odown_ref,
-    yacc, dacc, dus, mine, acc, via, last, zs, sems_s, sems_r, own_sem,
+    x1_in, dm_ref, g_ref, slope_ref, wu_ref, wd_ref, h2t_in, vec_ref, gdown_ref,
+    y_ref, dx1_ref, da_ref, gup_ref, sums_ref, odown_ref,
+    x1_ref, h2t_ref, in_sem, yacc, dacc, dus, mine, acc, via, last, zs, sems_s, sems_r, own_sem,
 ):
     step = pl.program_id(0)
     here = where_am_i()
@@ -935,8 +953,12 @@
             here, (sems_s, sems_r), i * Scatter.COPIES, gdown_ref.at[EVERY, TWO, TWO, down_rows(i, 1 - c), cols],
             lambda a, b, d, i=i: mine[i, a, b, d], acc.at[i], via.at[i], last.at[i], zs.at[i],
         ))
+    later = [
+        pltpu.make_async_copy(a, b, in_sem.at[n])
+        for n, (a, b) in enumerate(((h2t_in, h2t_ref), (x1_in, x1_ref)))
+    ]
     entries = [
-        (5.0 + PACE * i + lag, (i, phase)) for i in range(N_DOWN) for phase, lag in enumerate(BACK_LAG) if (i, phase) != (0, 0)
+        (5.0 + FFN_PACE * i + lag, (i, phase)) for i in range(N_DOWN) for phase, lag in enumerate(FFN_LAG) if (i, phase) != (0, 0)
     ]
     table, late = plan(entries, FFN_TICKS)
 
@@ -960,13 +982,13 @@
     @pl.when(step == 0)
     def _():
         say_hello(here)
-        for copy in own:
+        for copy in (*later, *own):
             copy.start()
 
         @pl.loop(0, T // MB)
         def _(i):
             rows = rows_of(i)
-            yacc[rows, :] = x1_ref[rows, :] + vec_ref[BD:BD + 1, :]
+            yacc[rows, :] = jnp.broadcast_to(vec_ref[BD:BD + 1, :], (MB, D))
             dacc[rows, :] = jnp.zeros((MB, D), F32)
         sums_ref[...] = jnp.zeros_like(sums_ref)
         sums_ref[2:3, :] = jnp.sum(dm_ref[...].astype(F32), 0, keepdims=True)
@@ -988,6 +1010,10 @@
         sums_ref[pl.ds(3 + step, 1), :] += jnp.sum(du.astype(F32), 0, keepdims=True)
         dacc[rows, :] += mm(du, wu_ref[...], NT)
 
+    @pl.when(step == 0)
+    def _():
+        later[0].wait()
+
     @pl.loop(0, 2)
     def _(t):
         tick(6 * step + 4 + t)
@@ -996,15 +1022,20 @@
 
     @pl.when(step == N_UP - 1)
     def _():
+        later[1].wait()
+
         @pl.loop(0, T // MB)
         def _(i):
             rows = rows_of(i)
-            n2, s2 = norm_parts(x1_ref[rows, :])
+            x1 = x1_ref[rows, :]
+            n2, s2 = norm_parts(x1)
             dh = dacc[rows, :]
             sums_ref[0:1, :] += jnp.sum(dh * n2, 0, keepdims=True)
             sums_ref[1:2, :] += jnp.sum(dh, 0, keepdims=True)
-            dx1_ref[rows, :] = dm_ref[rows, :].astype(F32) + norm_pull(dh, n2, s2, vec_ref[G2:G2 + 1, :])
-            y_ref[rows, :] = yacc[rows, :].astype(BF)
+            dx1 = dm_ref[rows, :].astype(F32) + norm_pull(dh, n2, s2, vec_ref[G2:G2 + 1, :])
+            dx1_ref[rows, :] = dx1
+            da_ref[rows, :] = dx1.astype(BF)
+            y_ref[rows, :] = (x1 + yacc[rows, :]).astype(BF)
         for action in late:
             act(action)
         for item in items:
@@ -1018,17 +1049,20 @@
         ffn_back_kernel,
         grid=(N_UP,),
         in_specs=[
-            fixed((T, D)), fixed((T, D)), col, col,
+            hbm(), fixed((T, D)), col, col,
             pl.BlockSpec((D, D), lambda s: (0, s)), pl.BlockSpec((D, D), lambda s: (s, 0)),
-            fixed((D, T)), fixed((NV, D)), hbm(),
+            hbm(), fixed((NV, D)), hbm(),
         ],
         out_specs=[
-            fixed((T, D)), fixed((T, D)), pl.BlockSpec((D, D), lambda s: (0, s)), fixed((8, D)), fixed((96, D)),
+            fixed((T, D)), fixed((T, D)), fixed((T, D)), pl.BlockSpec((D, D), lambda s: (0, s)), fixed((8, D)),
+            fixed((96, D)),
         ],
         out_shape=[
-            shape((T, D), BF), shape((T, D), F32), shape((D, FF), BF), shape((8, D), F32), shape((96, D), F32),
+            shape((T, D), BF), shape((T, D), F32), shape((T, D), BF), shape((D, FF), BF), shape((8, D), F32),
+            shape((96, D), F32),
         ],
         scratch_shapes=[
+            pltpu.VMEM((T, D), F32), pltpu.VMEM((D, T), BF), *dma_sems(2),
             pltpu.VMEM((T, D), F32), pltpu.VMEM((T, D), F32), pltpu.VMEM((T, D), BF),
             pltpu.VMEM((N_DOWN, NZ, 2, 2, CH, HW), BF), *scatter_bufs(N_DOWN, HW),
             *dma_sems(N_DOWN * 7, N_DOWN * 7, N_DOWN),
@@ -1044,12 +1078,12 @@
 
 
 def attn_back_kernel(
-    xb_ref, yb_ref, dx1_ref, h1t_ref, qkv_ref, p_ref, attn_ref, rl_ref, wo_ref, wqkv_ref, vec_ref, sums_ref, gup_ref,
+    xb_in, yb_in, dx1_in, da_ref, h1t_in, qkv_ref, p_ref, attn_ref, rl_ref, wo_ref, wqkv_ref, vec_ref, sums_ref, gup_ref,
     out_ref, gx_ref, oqkv_ref, oout_ref, oup_ref, *refs,
 ):
     small_outs = refs[:NV + 1]
     (
-        da, dos, dqkv, dh1, gqkv, gout, mine, acc, via, last, zs, done, landed, small,
+        xb_ref, yb_ref, dx1_ref, h1t_ref, in_sem, dos, dqkv, dh1, gqkv, gout, mine, acc, via, last, zs, done, landed, small,
         sems_s, sems_r, fin_s, fin_r, small_s, small_r, own_sem,
     ) = refs[NV + 1:]
     step = pl.program_id(0)
@@ -1073,6 +1107,11 @@
         items.append(Scatter(
             here, (sems_s, sems_r), n * Scatter.COPIES, theirs, get, acc.at[n], via.at[n], last.at[n], zs.at[n]))
 
+    later = [
+        pltpu.make_async_copy(a, b, in_sem.at[n])
+        for n, (a, b) in enumerate(((h1t_in, h1t_ref), (xb_in, xb_ref), (dx1_in, dx1_ref), (yb_in, yb_ref)))
+    ]
+
     def final(n):
         theirs = pl.ds(pl.multiple_of((1 - c) * 24, 8), 24)
         return remote(done.at[n, theirs], landed.at[n], (fin_s, fin_r), n, peers[5])
@@ -1127,7 +1166,7 @@
     @pl.when(step == 0)
     def _():
         say_hello(here)
-        for copy in own:
+        for copy in (*own, *later):
             copy.start()
         small[0] = jnp.zeros((16, D), F32)
         src = lax.broadcasted_iota(jnp.int32, (128, D), 0)
@@ -1137,8 +1176,7 @@
         @pl.loop(0, T // MB)
         def _(i):
             rows = rows_of(i)
-            d = dx1_ref[rows, :].astype(BF)
-            da[rows, :] = d
+            d = da_ref[rows, :]
             rl = lax.dot_general(
                 rl_ref[rows, :], spread, NN, precision=lax.Precision.HIGHEST, preferred_element_type=F32)
             small[0, 4:5, :] += jnp.sum(d.astype(F32), 0, keepdims=True)
@@ -1146,7 +1184,7 @@
             dh1[rows, :] = jnp.zeros((MB, D), F32)
         @pl.loop(0, 2)
         def _(t):
-            part = mm(attn_ref[:, pl.ds(pl.multiple_of(t * 384, 128), 384)], da[...], TN)
+            part = mm(attn_ref[:, pl.ds(pl.multiple_of(t * 384, 128), 384)], da_ref[...], TN)
             gout[pl.ds(2 * t, 2)] = part.astype(BF).reshape(2, 2, 2, CH, D)
 
         await_all()
@@ -1177,6 +1215,10 @@
         for n, part in enumerate((dq * scale, dk * scale, dv)):
             dqkv[rows, at + 128 * n:at + 128 * (n + 1)] = part.astype(BF)
 
+    @pl.when(step == 1)
+    def _():
+        later[0].wait()
+
     @pl.when(r == 1)
     def _():
         sums = jnp.sum(dqkv[...].astype(F32), 0, keepdims=True)
@@ -1202,6 +1244,8 @@
     @pl.when(step == N_ATT - 1)
     def _():
         rest = final_steps[1:]
+        for copy in later[1:]:
+            copy.wait()
 
         @pl.loop(0, T // MB)
         def _(i):
@@ -1223,7 +1267,7 @@
             n1, s1 = norm_parts(xb_ref[rr, :].astype(F32))
             small[0, 0:1, :] += jnp.sum(dh * n1, 0, keepdims=True)
             small[0, 1:2, :] += jnp.sum(dh, 0, keepdims=True)
-            da[rr, :] = (dx1_ref[rr, :] + norm_pull(dh, n1, s1, vec_ref[G1:G1 + 1, :])).astype(BF)
+            xb_ref[rr, :] = (dx1_ref[rr, :] + norm_pull(dh, n1, s1, vec_ref[G1:G1 + 1, :])).astype(BF)
         small[0, 5:12, :] = sums_ref[0:7, :]
         copies = []
 
@@ -1240,7 +1284,7 @@
                 act(rest.pop(0))
             if level == 0:
                 for row in range(2):
-                    rows_out(da, gx_ref, row)
+                    rows_out(xb_ref, gx_ref, row)
             if level == 1:
                 for row in range(2):
                     rows_out(yb_ref, out_ref, row)
@@ -1283,14 +1327,14 @@
             copy.wait_send()
 
 
-def attn_back(x, yb, dx1, h1t, qkv, p, attn, rl, watt, vec, sums, gup):
+def attn_back(x, yb, dx1, da, h1t, qkv, p, attn, rl, watt, vec, sums, gup):
     shape = jax.ShapeDtypeStruct
     n_fin = N_BACK
     return pl.pallas_call(
         attn_back_kernel,
         grid=(N_ATT,),
         in_specs=[
-            fixed((T, D)), fixed((T, D)), fixed((T, D)), fixed((D, T)), pl.BlockSpec((T, GW), lambda s: (0, s // 2)),
+            hbm(), hbm(), hbm(), fixed((T, D)), hbm(), pl.BlockSpec((T, GW), lambda s: (0, s // 2)),
             pl.BlockSpec((1, HG, S, S), lambda s: (s % 2, s // 2, 0, 0)), fixed((T, D)), fixed((T, 128)),
             pl.BlockSpec((D, D), lambda s: (0, 3), pipeline_mode=pl.Buffered(1)),
             pl.BlockSpec((D, GW), lambda s: (0, s // 2)), fixed((NV, D)), fixed((8, D)), hbm(),
@@ -1304,7 +1348,8 @@
             shape((24, FF), F32), *[shape((w,), F32) for w in VW],
         ],
         scratch_shapes=[
-            pltpu.VMEM((T, D), BF), pltpu.VMEM((T, D), BF), pltpu.VMEM((T, GW), BF), pltpu.VMEM((T, D), F32),
+            pltpu.VMEM((T, D), BF), pltpu.VMEM((T, D), BF), pltpu.VMEM((T, D), F32), pltpu.VMEM((D, T), BF), *dma_sems(4),
+            pltpu.VMEM((T, D), BF), pltpu.VMEM((T, GW), BF), pltpu.VMEM((T, D), F32),
             pltpu.VMEM((3, NZ, 2, 2, CH, GW), BF), pltpu.VMEM((NZ, 2, 2, CH, D), BF),
             pltpu.VMEM((N_UP, NZ, 2, 2, CH, HW), BF), *scatter_bufs(N_BACK, HW),
             pltpu.VMEM((N_BACK, CH, HW), F32), pltpu.VMEM((N_BACK, 24, HW), F32), pltpu.VMEM((10, 16, D), F32),
@@ -1312,21 +1357,31 @@
         ],
         compiler_params=pltpu.CompilerParams(collective_id=2, has_side_effects=True, vmem_limit_bytes=LIMIT),
         name="attention_back",
-    )(x, yb, dx1, h1t, qkv, p, attn, rl, watt, watt, vec, sums, gup.reshape(NZ, 2, 2, CH, FF))
+    )(x, yb, dx1, da, h1t, qkv, p, attn, rl, watt, watt, vec, sums, gup.reshape(NZ, 2, 2, CH, FF))
 
 
 def hand_over_kernel(*refs):
-    n = len(refs) // 2
+    n = (len(refs) - 2) // 3
+    sems_in, sems_out = refs[-2:]
+    held = refs[2 * n:3 * n]
+    arrive = [pltpu.make_async_copy(refs[i], held[i], sems_in.at[i]) for i in range(n)]
+    leave = [pltpu.make_async_copy(held[i], refs[n + i], sems_out.at[i]) for i in range(n)]
+    for copy in arrive:
+        copy.start()
     for i in range(n):
-        refs[n + i][...] = refs[i][...]
+        arrive[i].wait()
+        leave[i].start()
+    for copy in leave:
+        copy.wait()
 
 
 def hand_over(values):
     return pl.pallas_call(
         hand_over_kernel,
-        in_specs=[vmem()] * len(values),
-        out_specs=[vmem()] * len(values),
+        in_specs=[hbm()] * len(values),
+        out_specs=[hbm()] * len(values),
         out_shape=[jax.ShapeDtypeStruct(v.shape, v.dtype) for v in values],
+        scratch_shapes=[*[pltpu.VMEM(v.shape, v.dtype) for v in values], *dma_sems(len(values), len(values))],
         compiler_params=pltpu.CompilerParams(vmem_limit_bytes=LIMIT),
         name="results",
     )(*values)
@@ -1344,9 +1399,9 @@
     x, dm = inputs.transpose(1, 0, 2), out_grad.transpose(1, 0, 2)
     h1t, qkv, p, attn, rl, x1, dmp, h2t, g, slope, gdown, vec, xb, watt, wup, down = forward(
         row_kind, x, dm, w_qkv, w_out, w_up, w_down, (*vectors, b_up))
-    yb, dx1, gup, sums, gdown = ffn_back(
+    yb, dx1, da, gup, sums, gdown = ffn_back(
         x1, dmp, g, slope, wup.reshape(D, FF), down.reshape(FF, D), h2t, vec, gdown)
-    results = attn_back(xb, yb, dx1, h1t, qkv, p, attn, rl, watt.reshape(D, UP_AT), vec, sums, gup)
+    results = attn_back(xb, yb, dx1, da, h1t, qkv, p, attn, rl, watt.reshape(D, UP_AT), vec, sums, gup)
     out, gx, gqkv, gout, gup, gdown, *small = hand_over((*results[:5], gdown, *results[5:]))
     return out.transpose(1, 0, 2), gx.transpose(1, 0, 2), gqkv, gout, gup, gdown, small[:NV], small[NV]
 

time: 241 us -> 230 us (0.954)
  Pallas kernels: 240 us -> 229 us
    pallas_call x3, Pallas kernels: 136 us -> 129 us  [the longest x1 80.5 us: attn_back(): pl.pallas_call(attn_back_kernel, grid=(N_ATT,), in_specs=[hbm(), hbm(), h...]
    pallas_call x1, Pallas kernels: 104 us -> 99.9 us  [forward(): pl.pallas_call(forward_kernel, grid=(N_ATT + N_UP,), in_specs=[pl.BlockSp...]
where the time goes in v1:
time: 230 us
  Pallas kernels  229 us (100%)
    pallas_call x1, Pallas kernels, forward(): pl.pallas_call(forward_kernel, grid=(N_ATT + N_UP,), in_specs=[pl.BlockSp...  99.9 us
    pallas_call x1, Pallas kernels, attn_back(): pl.pallas_call(attn_back_kernel, grid=(N_ATT,), in_specs=[hbm(), hbm(), h...  80.5 us
    pallas_call x1, Pallas kernels, ffn_back(): pl.pallas_call(ffn_back_kernel, grid=(N_UP,), in_specs=[hbm(), fixed((T,...  45 us

profile of v1, /device:TPU:0, one launch (start us, length us, event | category | flops | bytes accessed | tf_op | source)
XLA Modules:
  0.0 229.9 jit_solution(1239254720252293759)
XLA Ops:
  0.7 99.9 %forward.1 = (bf16[768,1088]{1,0:T(8,128)(2,1)}, bf16[1088,2304]{1,0:T(8,128)(2,1)}, bf16[2,12,544,544]{3,2,1,0:T(8,128)(2,1)}, bf16[1088,768]{1,0:T(8,128)(2,1)...) custom-call(s32[2]{0:T(128)} %kind_ref.1, ...), custom_call_target="tpu_custom_call" | custom-call | tf_op jit(solution)/shard_map/forward/pallas_call | solution.py:898
  100.5 45.0 %feed_forward_back.1 = (bf16[1088,768]{1,0:T(8,128)(2,1)}, f32[1088,768]{1,0:T(8,128)}, bf16[1088,768]{1,0:T(8,128)(2,1)}, bf16[768,3072]{1,0:T(8,128)(2,1)}, f32[8,768]{1,0:T(8,128)}, /*index=5*/f32[96,768]{1,0:T(8,128)}) custom-call(f32[1088,768]{1,0:T(8,128)} %get-tuple-element.67.x1_in, bf16[1088,768]{1,0:T(8,128)(2,1)} %get-tuple-element.68.dm_ref, ...), custom_call_target="tpu_custom_call" | custom-call | tf_op jit(solution)/shard_map/feed_forward_back/pallas_call | solution.py:1048
  145.5 80.5 %attention_back.1 = (bf16[529,2,768]{2,1,0:T(2,128)(2,1)}, bf16[529,2,768]{2,1,0:T(2,128)(2,1)}, f32[24,2304]{1,0:T(8,128)}, f32[24,768]{1,0:T(8,128)}, f32[24,3...) custom-call(bf16[1088,768]{1,0:T(8,128)(2,1)} %get-tuple-element.66., ...), custom_call_target="tpu_custom_call" | custom-call | tf_op jit(solution)/shard_map/attention_back/pallas_call | solution.py:1333
  226.1 3.7 %results.1 = (bf16[529,2,768]{2,1,0:T(2,128)(2,1)}, bf16[529,2,768]{2,1,0:T(2,128)(2,1)}, f32[24,2304]{1,0:T(8,128)}, f32[24,768]{1,0:T(8,128)}, f32[24,3072]{1,...) custom-call(bf16[529,2,768]{2,1,0:T(2,128)(2,1)} %get-tuple-element., ...), custom_call_target="tpu_custom_call" | custom-call | tf_op jit(solution)/shard_map/results/pallas_call | solution.py:1379

commit v2 on v1

--- a/solution.py
+++ b/solution.py
@@ -610,21 +610,21 @@
 
 N_ATT = 2 * (D // QW)
 PACE = 5.4
-FORWARD_LAG = (0.0, 8.0, 20.0, 28.0, 34.0)
-FORWARD_FROM = 26.0
-FIRST_PACE = 3.6
+FORWARD_LAG = (0.0, 10.0, 24.0, 33.0, 40.0)
+FORWARD_FROM = 28.0
+FIRST_PACE = 3.2
 FORWARD_PACE = 5.4
 FORWARD_TICKS = [FORWARD_FROM + 2.9 * n for n in range(12)] + [FORWARD_FROM + 35.0 + 2.1 * n for n in range(16)]
 
 
 def forward_kernel(
-    kind_ref, x_ref, dm_ref, wqkv_ref, wout_ref, wup_ref, wdown_ref, *refs,
+    kind_ref, x_in, dm_in, wqkv_ref, wout_ref, wup_ref, wdown_ref, *refs,
 ):
     small_refs = refs[:NV + 1]
     (
         h1t_out, qkv_ref, p_ref, attn_out, rl_out, x1_out, dmp_out, h2t_out, g_ref, slope_ref, gdown_ref,
         vec_ref, xb_out, watt_out, wup_out, down_out,
-        h1t_ref, attn_ref, rl_ref, x1_ref, dmp_ref, h2t_ref, xb_ref, out_sem,
+        h1t_ref, attn_ref, rl_ref, x1_ref, dmp_ref, h2t_ref, xb_ref, out_sem, x_ref, dm_ref, in_sem,
         fa, fb, h1, h2, staged, swap, watt, wup, bqkv, bu, smalls,
         sems_s, sems_r, swap_s, swap_r, small_s, small_r, copy_sem,
     ) = refs[NV + 1:]
@@ -656,6 +656,8 @@
         keeps.append(pltpu.make_async_copy(
             src.at[:, :, :, :, cols], dst.at[:, :, :, :, cols], copy_sem.at[i]))
 
+    x_load = pltpu.make_async_copy(x_in, x_ref, in_sem.at[0])
+    dm_load = pltpu.make_async_copy(dm_in, dm_ref, in_sem.at[1])
     first_out = [
         pltpu.make_async_copy(a, b, out_sem.at[n])
         for n, (a, b) in enumerate(((h1t_ref, h1t_out), (dmp_ref, dmp_out), (xb_ref, xb_out)))
@@ -697,6 +699,8 @@
     @pl.when(step == 0)
     def _():
         say_hello(here)
+        x_load.start()
+        dm_load.start()
         for pair in range(6):
             for n in range(3):
                 at = pair * 384 + n * 128
@@ -744,6 +748,7 @@
             copy.start()
         for i in range(1, N_WIDE):
             take_block(i)
+        x_load.wait()
         rows_in(x_ref, 0, x1_ref, xb_ref)
         for copy in small_z:
             copy.wait_recv()
@@ -756,6 +761,7 @@
         act_some(1)
         items[0].start(2)
         act_some(1)
+        dm_load.wait()
         for row in range(2):
             rows_in(dm_ref, row, dmp_ref)
         items[0].start(3)
@@ -899,7 +905,7 @@
         forward_kernel,
         grid=(N_ATT + N_UP,),
         in_specs=[
-            pl.BlockSpec(memory_space=pltpu.SMEM), fixed((SEQ, 2, D)), fixed((SEQ, 2, D)),
+            pl.BlockSpec(memory_space=pltpu.SMEM), hbm(), hbm(),
             fixed((24, 3 * D)), fixed((24, D)), fixed((24, FF)), fixed((1, 1, 1, 96, D)),
             *[pl.BlockSpec((w,), lambda s: (0,), pipeline_mode=pl.Buffered(1)) for w in VW],
         ],
@@ -920,6 +926,7 @@
         scratch_shapes=[
             pltpu.VMEM((D, T), BF), pltpu.VMEM((T, D), BF), pltpu.VMEM((T, 128), F32), pltpu.VMEM((T, D), F32),
             pltpu.VMEM((T, D), BF), pltpu.VMEM((D, T), BF), pltpu.VMEM((T, D), BF), *dma_sems(7),
+            pltpu.VMEM((SEQ, 2, D), BF), pltpu.VMEM((SEQ, 2, D), BF), *dma_sems(2),
             pltpu.VMEM((2, S, 128), BF), pltpu.VMEM((2, S, 128), BF), pltpu.VMEM((T, D), BF), pltpu.VMEM((T, D), BF),
             pltpu.VMEM((24, AW), F32), pltpu.VMEM((24, AW // 2), F32),
             pltpu.VMEM((NZ, 2, 2, CH, UP_AT), BF), pltpu.VMEM((NZ, 2, 2, CH, FF), BF),
@@ -1079,11 +1086,11 @@
 
 def attn_back_kernel(
     xb_in, yb_in, dx1_in, da_ref, h1t_in, qkv_ref, p_ref, attn_ref, rl_ref, wo_ref, wqkv_ref, vec_ref, sums_ref, gup_ref,
-    out_ref, gx_ref, oqkv_ref, oout_ref, oup_ref, *refs,
+    out_hbm, gx_hbm, oqkv_ref, oout_ref, oup_ref, *refs,
 ):
     small_outs = refs[:NV + 1]
     (
-        xb_ref, yb_ref, dx1_ref, h1t_ref, in_sem, dos, dqkv, dh1, gqkv, gout, mine, acc, via, last, zs, done, landed, small,
+        xb_ref, yb_ref, dx1_ref, h1t_ref, in_sem, out_ref, gx_ref, out_sem, dos, dqkv, dh1, gqkv, gout, mine, acc, via, last, zs, done, landed, small,
         sems_s, sems_r, fin_s, fin_r, small_s, small_r, own_sem,
     ) = refs[NV + 1:]
     step = pl.program_id(0)
@@ -1111,6 +1118,9 @@
         pltpu.make_async_copy(a, b, in_sem.at[n])
         for n, (a, b) in enumerate(((h1t_in, h1t_ref), (xb_in, xb_ref), (dx1_in, dx1_ref), (yb_in, yb_ref)))
     ]
+
+    y_out = pltpu.make_async_copy(out_ref, out_hbm, out_sem.at[0])
+    gx_out = pltpu.make_async_copy(gx_ref, gx_hbm, out_sem.at[1])
 
     def final(n):
         theirs = pl.ds(pl.multiple_of((1 - c) * 24, 8), 24)
@@ -1277,46 +1287,45 @@
             copies.append(copy)
 
         send_small(0, 0, 1, peers[5])
-        hops = [(1, 2, 3, peers[3]), (2, 4, 5, peers[4])]
-        level = 0
-        while rest or level < 4:
-            if rest:
-                act(rest.pop(0))
-            if level == 0:
-                for row in range(2):
-                    rows_out(xb_ref, gx_ref, row)
-            if level == 1:
-                for row in range(2):
-                    rows_out(yb_ref, out_ref, row)
-            if level < 2:
-                copies[level].wait_recv()
-                small[2 * level + 2] = small[2 * level] + small[2 * level + 1]
-                send_small(*hops[level])
-            elif level == 2:
-                copies[2].wait_recv()
-                small[6] = small[4] + small[5]
-                for k in range(3):
-                    send_small(3 + k, 6, 7 + k, peers[k])
-            elif level == 3:
-                for k in range(3):
-                    copies[3 + k].wait_recv()
-                total = small[6] + small[7] + small[8] + small[9]
-                me = lax.axis_index("dp") * lax.axis_size("fsdp") + lax.axis_index("fsdp")
-                src = lax.broadcasted_iota(jnp.int32, (D, 128), 0)
-                dst = lax.broadcasted_iota(jnp.int32, (D, 128), 1)
-
-                def pick(lines, width, at):
-                    chosen = jnp.where((src == at + dst) & (dst < width), 1.0, 0.0)
-                    return lax.dot_general(
-                        lines, chosen, NN, precision=lax.Precision.HIGHEST, preferred_element_type=F32)
-
-                mine_of = pick(total[:8], 24, me * 24)
-                for n in range(NV):
-                    small_outs[n][...] = mine_of[n, :24]
-                row = lax.broadcasted_iota(jnp.int32, (8, D), 0)
-                longest = jnp.sum(jnp.where(row == lax.div(me, 8), total[8:16], 0.0), 0, keepdims=True)
-                small_outs[NV][...] = pick(jnp.broadcast_to(longest, (8, D)), 96, lax.rem(me, 8) * 96)[0, :96]
-            level += 1
+        act(rest.pop(0))
+        copies[0].wait_recv()
+        small[2] = small[0] + small[1]
+        send_small(1, 2, 3, peers[3])
+        for row in range(2):
+            rows_out(xb_ref, gx_ref, row)
+        gx_out.start()
+        copies[1].wait_recv()
+        small[4] = small[2] + small[3]
+        send_small(2, 4, 5, peers[4])
+        act(rest.pop(0))
+        for row in range(2):
+            rows_out(yb_ref, out_ref, row)
+        y_out.start()
+        copies[2].wait_recv()
+        small[6] = small[4] + small[5]
+        for k in range(3):
+            send_small(3 + k, 6, 7 + k, peers[k])
+        for k in range(3):
+            copies[3 + k].wait_recv()
+        total = small[6] + small[7] + small[8] + small[9]
+        me = lax.axis_index("dp") * lax.axis_size("fsdp") + lax.axis_index("fsdp")
+        src = lax.broadcasted_iota(jnp.int32, (D, 128), 0)
+        dst = lax.broadcasted_iota(jnp.int32, (D, 128), 1)
+
+        def pick(lines, width, at):
+            chosen = jnp.where((src == at + dst) & (dst < width), 1.0, 0.0)
+            return lax.dot_general(
+                lines, chosen, NN, precision=lax.Precision.HIGHEST, preferred_element_type=F32)
+
+        mine_of = pick(total[:8], 24, me * 24)
+        for n in range(NV):
+            small_outs[n][...] = mine_of[n, :24]
+        row = lax.broadcasted_iota(jnp.int32, (8, D), 0)
+        longest = jnp.sum(jnp.where(row == lax.div(me, 8), total[8:16], 0.0), 0, keepdims=True)
+        small_outs[NV][...] = pick(jnp.broadcast_to(longest, (8, D)), 96, lax.rem(me, 8) * 96)[0, :96]
+        act(rest.pop(0))
+        gx_out.wait()
+        y_out.wait()
         for n in range(N_BACK):
             copy = final(n)
             copy.wait_recv()
@@ -1340,7 +1349,7 @@
             pl.BlockSpec((D, GW), lambda s: (0, s // 2)), fixed((NV, D)), fixed((8, D)), hbm(),
         ],
         out_specs=[
-            fixed((SEQ, 2, D)), fixed((SEQ, 2, D)), fixed((24, 3 * D)), fixed((24, D)), fixed((24, FF)),
+            hbm(), hbm(), fixed((24, 3 * D)), fixed((24, D)), fixed((24, FF)),
             *[pl.BlockSpec((w,), lambda s: (0,), pipeline_mode=pl.Buffered(1)) for w in VW],
         ],
         out_shape=[
@@ -1349,6 +1358,7 @@
         ],
         scratch_shapes=[
             pltpu.VMEM((T, D), BF), pltpu.VMEM((T, D), BF), pltpu.VMEM((T, D), F32), pltpu.VMEM((D, T), BF), *dma_sems(4),
+            pltpu.VMEM((SEQ, 2, D), BF), pltpu.VMEM((SEQ, 2, D), BF), *dma_sems(2),
             pltpu.VMEM((T, D), BF), pltpu.VMEM((T, GW), BF), pltpu.VMEM((T, D), F32),
             pltpu.VMEM((3, NZ, 2, 2, CH, GW), BF), pltpu.VMEM((NZ, 2, 2, CH, D), BF),
             pltpu.VMEM((N_UP, NZ, 2, 2, CH, HW), BF), *scatter_bufs(N_BACK, HW),

time: 230 us -> 228 us (level)
    pallas_call x1, Pallas kernels: 99.9 us -> 97.5 us  [forward(): pl.pallas_call(forward_kernel, grid=(N_ATT + N_UP,), in_specs=[pl.BlockSp...]
where the time goes in v2:
time: 228 us
  Pallas kernels  227 us (100%)
    pallas_call x1, Pallas kernels, forward(): pl.pallas_call(forward_kernel, grid=(N_ATT + N_UP,), in_specs=[pl.BlockSp...  97.5 us
    pallas_call x1, Pallas kernels, attn_back(): pl.pallas_call(attn_back_kernel, grid=(N_ATT,), in_specs=[hbm(), hbm(), h...  80.6 us
    pallas_call x1, Pallas kernels, ffn_back(): pl.pallas_call(ffn_back_kernel, grid=(N_UP,), in_specs=[hbm(), fixed((T,...  45.4 us

profile of v2, /device:TPU:0, one launch (start us, length us, event | category | flops | bytes accessed | tf_op | source)
XLA Modules:
  0.0 228.1 jit_solution(9143796281894202110)
XLA Ops:
  0.7 97.5 %forward.1 = (bf16[768,1088]{1,0:T(8,128)(2,1)}, bf16[1088,2304]{1,0:T(8,128)(2,1)}, bf16[2,12,544,544]{3,2,1,0:T(8,128)(2,1)}, bf16[1088,768]{1,0:T(8,128)(2,1)...) custom-call(s32[2]{0:T(128)} %kind_ref.1, ...), custom_call_target="tpu_custom_call" | custom-call | tf_op jit(solution)/shard_map/forward/pallas_call | solution.py:904
  98.2 45.4 %feed_forward_back.1 = (bf16[1088,768]{1,0:T(8,128)(2,1)}, f32[1088,768]{1,0:T(8,128)}, bf16[1088,768]{1,0:T(8,128)(2,1)}, bf16[768,3072]{1,0:T(8,128)(2,1)}, f32[8,768]{1,0:T(8,128)}, /*index=5*/f32[96,768]{1,0:T(8,128)}) custom-call(f32[1088,768]{1,0:T(8,128)} %get-tuple-element.67.x1_in, bf16[1088,768]{1,0:T(8,128)(2,1)} %get-tuple-element.68.dm_ref, ...), custom_call_target="tpu_custom_call" | custom-call | tf_op jit(solution)/shard_map/feed_forward_back/pallas_call | solution.py:1055
  143.6 80.6 %attention_back.1 = (bf16[529,2,768]{2,1,0:T(2,128)(2,1)}, bf16[529,2,768]{2,1,0:T(2,128)(2,1)}, f32[24,2304]{1,0:T(8,128)}, f32[24,768]{1,0:T(8,128)}, f32[24,3...) custom-call(bf16[1088,768]{1,0:T(8,128)(2,1)} %get-tuple-element.66., ...), custom_call_target="tpu_custom_call" | custom-call | tf_op jit(solution)/shard_map/attention_back/pallas_call | solution.py:1342
  224.2 3.7 %results.1 = (bf16[529,2,768]{2,1,0:T(2,128)(2,1)}, bf16[529,2,768]{2,1,0:T(2,128)(2,1)}, f32[24,2304]{1,0:T(8,128)}, f32[24,768]{1,0:T(8,128)}, f32[24,3072]{1,...) custom-call(bf16[529,2,768]{2,1,0:T(2,128)(2,1)} %get-tuple-element., ...), custom_call_target="tpu_custom_call" | custom-call | tf_op jit(solution)/shard_map/results/pallas_call | solution.py:1389

commit v3 on v2

--- a/solution.py
+++ b/solution.py
@@ -1264,7 +1264,7 @@
                 for action in earlier[:-1]:
                     act(action)
 
-            @pl.when(i == 1)
+            @pl.when(i == 0)
             def _():
                 act(final_steps[0])
 

time: 228 us -> 228 us (level)
  no operation moved by 1% of the time
where the time goes in v3:
time: 228 us
  Pallas kernels  227 us (100%)
    pallas_call x1, Pallas kernels, forward(): pl.pallas_call(forward_kernel, grid=(N_ATT + N_UP,), in_specs=[pl.BlockSp...  97.5 us
    pallas_call x1, Pallas kernels, attn_back(): pl.pallas_call(attn_back_kernel, grid=(N_ATT,), in_specs=[hbm(), hbm(), h...  80.1 us
    pallas_call x1, Pallas kernels, ffn_back(): pl.pallas_call(ffn_back_kernel, grid=(N_UP,), in_specs=[hbm(), fixed((T,...  45.4 us

profile of v3, /device:TPU:0, one launch (start us, length us, event | category | flops | bytes accessed | tf_op | source)
XLA Modules:
  0.0 227.6 jit_solution(15307594222780851313)
XLA Ops:
  0.7 97.5 %forward.1 = (bf16[768,1088]{1,0:T(8,128)(2,1)}, bf16[1088,2304]{1,0:T(8,128)(2,1)}, bf16[2,12,544,544]{3,2,1,0:T(8,128)(2,1)}, bf16[1088,768]{1,0:T(8,128)(2,1)...) custom-call(s32[2]{0:T(128)} %kind_ref.1, ...), custom_call_target="tpu_custom_call" | custom-call | tf_op jit(solution)/shard_map/forward/pallas_call | solution.py:904
  98.2 45.4 %feed_forward_back.1 = (bf16[1088,768]{1,0:T(8,128)(2,1)}, f32[1088,768]{1,0:T(8,128)}, bf16[1088,768]{1,0:T(8,128)(2,1)}, bf16[768,3072]{1,0:T(8,128)(2,1)}, f32[8,768]{1,0:T(8,128)}, /*index=5*/f32[96,768]{1,0:T(8,128)}) custom-call(f32[1088,768]{1,0:T(8,128)} %get-tuple-element.67.x1_in, bf16[1088,768]{1,0:T(8,128)(2,1)} %get-tuple-element.68.dm_ref, ...), custom_call_target="tpu_custom_call" | custom-call | tf_op jit(solution)/shard_map/feed_forward_back/pallas_call | solution.py:1055
  143.6 80.1 %attention_back.1 = (bf16[529,2,768]{2,1,0:T(2,128)(2,1)}, bf16[529,2,768]{2,1,0:T(2,128)(2,1)}, f32[24,2304]{1,0:T(8,128)}, f32[24,768]{1,0:T(8,128)}, f32[24,3...) custom-call(bf16[1088,768]{1,0:T(8,128)(2,1)} %get-tuple-element.66., ...), custom_call_target="tpu_custom_call" | custom-call | tf_op jit(solution)/shard_map/attention_back/pallas_call | solution.py:1342
  223.7 3.7 %results.1 = (bf16[529,2,768]{2,1,0:T(2,128)(2,1)}, bf16[529,2,768]{2,1,0:T(2,128)(2,1)}, f32[24,2304]{1,0:T(8,128)}, f32[24,768]{1,0:T(8,128)}, f32[24,3072]{1,...) custom-call(bf16[529,2,768]{2,1,0:T(2,128)(2,1)} %get-tuple-element., ...), custom_call_target="tpu_custom_call" | custom-call | tf_op jit(solution)/shard_map/results/pallas_call | solution.py:1389
